TPU v7x, 32 devices: a whole 2x2x4 slice. The times are simulated.
32 devices in a mesh: ctx: 16 (over z, y, x), head: 2 (over core).
Axes of the slice: x: 2, y: 2, z: 4, core: 2. Of those that a mesh axis runs over, the one named last changes fastest.
Arguments:
- tokens: bfloat16 [16384, 2048], P('ctx', 'head'), may hold values from -6 to 6
- w_qkv: bfloat16 [3, 2048, 2048], P(None, 'ctx', 'head'), may hold values from -0.125 to 0.125
- out_gain: float32 [2048], P('head'), may hold values from 0.25 to 1.75
- seg_ids: int32 [16384], P('ctx'), may hold values from 0 to 15, never falling along the last dimension, each value on 1 to 4096 neighbouring positions
Outputs:
- attended: bfloat16 [16384, 2048], P('ctx', 'head')
Inputs may be any that keep to these rules, and one draw needn't show every extreme that they name: `seg_ids`: segment numbers never fall along the stream; each segment covers 1 to 4096 consecutive tokens, and one covers exactly 4096.
All inputs are finite; a program needn't handle non-finite values.
Results may differ from a plain program's by a relative error of at most 0.012.
Values may be sent and summed in bfloat16 or wider, within the bound.
A program may use at most 64 MiB of HBM per device.

v0:
```python
import jax
import jax.numpy as jnp
from jax import lax
from jax.sharding import PartitionSpec as P

HEAD_DIM = 128


def passed_along(value, axis, steps):
    count = lax.axis_size(axis)
    leading, last = (max(0, -steps), min(count, count - steps))
    return lax.ppermute(value, axis, [(source, source + steps) for source in range(leading, last)])


def feature_map(values):
    return (jax.nn.elu(values.astype(jnp.float32)) + 1.0).astype(jnp.bfloat16)


def combine(earlier, later):
    first_state, first_tail = earlier
    later_state, later_tail = later
    linked = (first_tail == later_tail) | (later_tail < 0.0)
    return (
        later_state + jnp.where(linked, first_state, 0.0),
        jnp.where(later_tail < 0.0, first_tail, later_tail),
    )


def prepare(projected, segment):
    row_count = segment.shape[0]
    head_count = projected.shape[2] // HEAD_DIM
    queries = feature_map(projected[0]).reshape(row_count, head_count, HEAD_DIM)
    key_map = feature_map(projected[1]).reshape(row_count, head_count, HEAD_DIM)
    values = projected[2].reshape(row_count, head_count, HEAD_DIM)
    seg_float = segment.astype(jnp.float32)
    tail_id = seg_float[-1]
    key_tail = jnp.where((seg_float == tail_id)[:, None, None], key_map, jnp.zeros_like(key_map))
    kv_state = jnp.einsum("thd,the->hde", key_tail, values, preferred_element_type=jnp.float32)
    return (queries, key_map, values, seg_float, kv_state, tail_id)


def complete(queries, key_map, values, seg_float, state_in, tail_in, out_gain):
    row_count, head_count = (queries.shape[0], queries.shape[1])
    state_low = state_in.astype(jnp.bfloat16)
    prefix = jnp.einsum("thd,hde->the", queries, state_low, preferred_element_type=jnp.float32)
    prefix = jnp.where((seg_float == tail_in)[:, None, None], prefix, 0.0)
    block_rows = min(512, row_count)
    positions = jnp.arange(row_count, dtype=jnp.int32)

    def one_block(blk_no):
        first_row = blk_no * block_rows
        query_blk = lax.dynamic_slice_in_dim(queries, first_row, block_rows, 0)
        query_pos = first_row + jnp.arange(block_rows, dtype=jnp.int32)
        query_seg = lax.dynamic_slice_in_dim(seg_float, first_row, block_rows, 0)
        scores = jnp.einsum("bhd,shd->hbs", query_blk, key_map, preferred_element_type=jnp.float32)
        visible = (positions[None, :] <= query_pos[:, None]) & (
            seg_float[None, :] == query_seg[:, None]
        )
        weights = jnp.where(visible[None], scores, 0.0).astype(jnp.bfloat16)
        return jnp.einsum("hbs,she->bhe", weights, values, preferred_element_type=jnp.float32)

    local_part = lax.map(one_block, jnp.arange(row_count // block_rows, dtype=jnp.int32))
    numerator = local_part.reshape(row_count, head_count, HEAD_DIM) + prefix
    inv_norm = lax.rsqrt(jnp.mean(numerator * numerator, axis=-1, keepdims=True) + 1e-05)
    result = numerator * inv_norm * out_gain.reshape(head_count, HEAD_DIM)
    return result.astype(jnp.bfloat16).reshape(row_count, head_count * HEAD_DIM)


def per_device(tokens, w_qkv, out_gain, seg_ids):
    whole = lax.all_gather(tokens, "head", axis=1, tiled=True)
    projected = jnp.einsum(
        "tr,grc->gtc",
        whole,
        lax.all_gather(w_qkv, "ctx", axis=1, tiled=True),
        preferred_element_type=jnp.float32,
    ).astype(jnp.bfloat16)
    queries, key_map, values, seg_float, kv_state, tail_id = prepare(projected, seg_ids)
    empty_state = jnp.zeros_like(kv_state)
    own_pair = (kv_state, tail_id)

    def hand_round(turn_no, carried):
        running, _ = carried
        incoming = (
            passed_along(running[0].astype(jnp.bfloat16), "ctx", 1).astype(jnp.float32),
            passed_along(running[1].astype(jnp.bfloat16), "ctx", 1).astype(jnp.float32),
        )
        return (combine(incoming, own_pair), incoming)

    start_pair = (empty_state, jnp.array(-1.0, jnp.float32))
    _, arrived = lax.fori_loop(0, lax.axis_size("ctx") - 1, hand_round, (own_pair, start_pair))
    state_in, tail_in = arrived
    return complete(queries, key_map, values, seg_float, state_in, tail_in, out_gain)


def solution(mesh):
    placed = (P("ctx", "head"), P(None, "ctx", "head"), P("head"), P("ctx"))
    return jax.shard_map(
        per_device, mesh=mesh, in_specs=placed, out_specs=P("ctx", "head"), check_vma=False
    )
```

profile of v0, /device:TPU:0, one launch (start us, length us, event | category | flops | bytes accessed | tf_op | source)
XLA Modules:
  0.0 608.0 jit_solution(14240363314814480759)
XLA Ops:
  11.9 13.4 %all-gather.5.cloned.1.call-done = bf16[1024,2048]{1,0:T(8,128)(2,1)} async-done(((bf16[1024,1024]{1,0:T(8,128)(2,1)}), bf16[1024,2048]{1,0:T(8,128)(2,1)}) %all-gather.5.cloned.1.call-update) | async-done | bytes 4194320 | tf_op jit(solution)/shard_map/all_gather | solution.py:70
  25.3 199.9 %all-gather.3.cloned.1.call-done = bf16[3,2048,1024]{1,2,0:T(8,128)(2,1)} async-done(((bf16[3,128,1024]{1,2,0:T(8,128)(2,1)}), bf16[3,2048,1024]{1,2,0:T(8,128)(2,1)}) %all-gather.3.cloned.1.call-update) | async-done | bytes 12582928 | tf_op jit(solution)/shard_map/all_gather | solution.py:74
  225.2 17.1 %convert_bitcast_fusion = bf16[3,1024,1024]{1,2,0:T(8,128)(2,1)S(1)} fusion(bf16[3,2048,1024]{1,2,0:T(8,128)(2,1)} %all-gather.3.cloned.1.call-done, bf16[1024,2048]{1,0:T(8,128)(2,1)} %all-gather.5.cloned.1.call-done), kind=kOutput, calls=%fused_computation.16 | convolution fusion | flops 12888047616 | bytes 23068672 | tf_op jit(solution)/shard_map/tr,grc->gtc/dot_general | solution.py:71
  251.8 7.0 %broadcast_select_fusion = (bf16[1024,8,128]{2,1,0:T(8,128)(2,1)S(1)}, bf16[1024,8,128]{2,1,0:T(8,128)(2,1)}) fusion(pred[1024]{0:T(1024)(128)(4,1)S(1)} %broadcast_compare_fusion.1, f32[1024,8,128]{2,1,0:T(8,128)} %copy.9), kind=kLoop, calls=%fused_computation.31 | loop fusion | flops 6291456 | bytes 8389632 | tf_op jit(solution)/shard_map/jit(_where)/select_n | solution.py:37
  259.8 210.6 %while.28 = (s32[]{:T(128)}, bf16[8,128,128]{2,1,0:T(8,128)(2,1)S(1)}, bf16[]{:T(256)}, bf16[8,128,128]{2,1,0:T(8,128)(2,1)}, f32[]{:T(128)}, /*index=5*/f32[]{:...) while((s32[]{:T(128)}, bf16[8,128,128]{2,1,0:T(8,128)(2,1)S(1)}, bf16[]{:T(256)}, ...), condition=%wide.region_3.4_spmd, body=%wide.region_2.3_spmd.sunk | while | flops 655366 | bytes 2359503 | solution.py:90
  263.2 5.8 collective-permute-start
  303.3 6.2 %collective-permute-start = (bf16[]{:T(256)}, bf16[]{:T(256)}, u32[]{:S(2)}, u32[]{:S(2)}) collective-permute-start(bf16[]{:T(256)} %get-tuple-element.319), channel_id=1, source_target_pairs={{0,2},{2,4},{4,6},{6,8},{8,10},{10,12},{12,14},{14,16},{16,18},{18... | collective-permute-start | bytes 14 | tf_op jit(solution)/shard_map/while/body/eval_jaxpr/ppermute | solution.py:12
  317.3 6.4 %collective-permute-start = (bf16[]{:T(256)}, bf16[]{:T(256)}, u32[]{:S(2)}, u32[]{:S(2)}) collective-permute-start(bf16[]{:T(256)} %get-tuple-element.319), channel_id=1, source_target_pairs={{0,2},{2,4},{4,6},{6,8},{8,10},{10,12},{12,14},{14,16},{16,18},{18... | collective-permute-start | bytes 14 | tf_op jit(solution)/shard_map/while/body/eval_jaxpr/ppermute | solution.py:12
  331.6 6.3 %collective-permute-start = (bf16[]{:T(256)}, bf16[]{:T(256)}, u32[]{:S(2)}, u32[]{:S(2)}) collective-permute-start(bf16[]{:T(256)} %get-tuple-element.319), channel_id=1, source_target_pairs={{0,2},{2,4},{4,6},{6,8},{8,10},{10,12},{12,14},{14,16},{16,18},{18... | collective-permute-start | bytes 14 | tf_op jit(solution)/shard_map/while/body/eval_jaxpr/ppermute | solution.py:12
  345.8 6.0 collective-permute-start
  359.6 6.0 collective-permute-start
  373.5 6.0 collective-permute-start
  387.4 6.0 collective-permute-start
  401.3 5.9 collective-permute-start
  415.1 6.0 collective-permute-start
  429.4 6.6 %collective-permute-start = (bf16[]{:T(256)}, bf16[]{:T(256)}, u32[]{:S(2)}, u32[]{:S(2)}) collective-permute-start(bf16[]{:T(256)} %get-tuple-element.319), channel_id=1, source_target_pairs={{0,2},{2,4},{4,6},{6,8},{8,10},{10,12},{12,14},{14,16},{16,18},{18... | collective-permute-start | bytes 14 | tf_op jit(solution)/shard_map/while/body/eval_jaxpr/ppermute | solution.py:12
  445.2 6.5 %collective-permute-start = (bf16[]{:T(256)}, bf16[]{:T(256)}, u32[]{:S(2)}, u32[]{:S(2)}) collective-permute-start(bf16[]{:T(256)} %get-tuple-element.319), channel_id=1, source_target_pairs={{0,2},{2,4},{4,6},{6,8},{8,10},{10,12},{12,14},{14,16},{16,18},{18... | collective-permute-start | bytes 14 | tf_op jit(solution)/shard_map/while/body/eval_jaxpr/ppermute | solution.py:12
  460.0 6.5 %collective-permute-start = (bf16[]{:T(256)}, bf16[]{:T(256)}, u32[]{:S(2)}, u32[]{:S(2)}) collective-permute-start(bf16[]{:T(256)} %get-tuple-element.319), channel_id=1, source_target_pairs={{0,2},{2,4},{4,6},{6,8},{8,10},{10,12},{12,14},{14,16},{16,18},{18... | collective-permute-start | bytes 14 | tf_op jit(solution)/shard_map/while/body/eval_jaxpr/ppermute | solution.py:12
  480.0 107.5 %while.29 = (s32[]{:T(128)}, f32[2,512,8,128]{1,0,3,2:T(2,128)}, s32[2]{0:T(128)S(1)}, f32[1024]{0:T(1024)S(1)}, bf16[1024,8,128]{2,1,0:T(8,128)(2,1)}, /*index=...) while((s32[]{:T(128)}, f32[2,512,8,128]{1,0,3,2:T(2,128)}, ...), condition=%wide.region_1.2_spmd.clone, body=%wide.region_0.1_spmd.clone.sunk | while | flops 2157445632 | bytes 18888888 | solution.py:62
  483.1 8.1 %fusion.43 = f32[1,512,8,128]{3,1,2,0:T(8,128)} fusion(bf16[1024,8,128]{2,0,1:T(8,128)(2,1)} %get-tuple-element.303, pred[512,1024]{1,0:T(8,128)(4,1)S(1)} %fusion.42, bf16[1024,8,128]{2,1,0:T(8,128)(2,1)} %get-tuple-element.302, bf16[512,8,128]{2,1,0:T(8,128)(2,1)S(1)} %constant_dynamic-slice_fusion.2), kind=kOutput, calls=%fused_computation.7.clone.1 | convolution fusion | flops 2155872256 | bytes 7864320 | tf_op jit(solution)/shard_map/while/body/eval_jaxpr/hbs,she->bhe/dot_general | solution.py:60
  495.9 37.9 %dynamic_update_slice.6 = f32[2,512,8,128]{1,0,3,2:T(2,128)} dynamic-update-slice(f32[2,512,8,128]{1,0,3,2:T(2,128)} %get-tuple-element.287, f32[1,512,8,128]{1,0,3,2:T(1,128)S(1)} %copy.49, s32[]{:T(128)} %get-tuple-element.286, s32[]{:T(128)} %constant.42.clone.1..sunk, s32[]{:T(128)} %constant.42.clone.1..sunk, s32[]{:T(128)} %constant.42.clone.1..sunk) | dynamic-update-slice | bytes 4194308 | tf_op jit(solution)/shard_map/while/body/jit(dynamic_update_index_in_dim)/dynamic_update_slice | solution.py:62
  536.9 8.1 %fusion.43 = f32[1,512,8,128]{3,1,2,0:T(8,128)} fusion(bf16[1024,8,128]{2,0,1:T(8,128)(2,1)} %get-tuple-element.303, pred[512,1024]{1,0:T(8,128)(4,1)S(1)} %fusion.42, bf16[1024,8,128]{2,1,0:T(8,128)(2,1)} %get-tuple-element.302, bf16[512,8,128]{2,1,0:T(8,128)(2,1)S(1)} %constant_dynamic-slice_fusion.2), kind=kOutput, calls=%fused_computation.7.clone.1 | convolution fusion | flops 2155872256 | bytes 7864320 | tf_op jit(solution)/shard_map/while/body/eval_jaxpr/hbs,she->bhe/dot_general | solution.py:60
  549.6 37.9 %dynamic_update_slice.6 = f32[2,512,8,128]{1,0,3,2:T(2,128)} dynamic-update-slice(f32[2,512,8,128]{1,0,3,2:T(2,128)} %get-tuple-element.287, f32[1,512,8,128]{1,0,3,2:T(1,128)S(1)} %copy.49, s32[]{:T(128)} %get-tuple-element.286, s32[]{:T(128)} %constant.42.clone.1..sunk, s32[]{:T(128)} %constant.42.clone.1..sunk, s32[]{:T(128)} %constant.42.clone.1..sunk) | dynamic-update-slice | bytes 4194308 | tf_op jit(solution)/shard_map/while/body/jit(dynamic_update_index_in_dim)/dynamic_update_slice | solution.py:62
  587.5 6.7 %reshape.87 = f32[1024,8,128]{0,2,1:T(8,128)} reshape(f32[2,512,8,128]{1,0,3,2:T(2,128)} %get-tuple-element.114) | data formatting | bytes 8388608 | tf_op jit(solution)/shard_map/reshape | solution.py:63
  (102 shorter events, 131.0 us)
Async XLA Ops:
  6.5 18.8 %all-gather.5.cloned.1.call-start = ((), (), s32[]{:S(2)}) async-start(), calls=%async_computation.1 | async-start | bytes 6291456 | tf_op jit(solution)/shard_map/all_gather | solution.py:70
  7.3 217.9 %all-gather.3.cloned.1.call-start = ((), (), s32[]{:S(2)}) async-start(), calls=%async_computation | async-start | bytes 13369344 | tf_op jit(solution)/shard_map/all_gather | solution.py:74
  259.8 12.2 %collective-permute-start.1 = (bf16[8,128,128]{2,1,0:T(8,128)(2,1)S(1)}, bf16[8,128,128]{2,1,0:T(8,128)(2,1)S(1)}, u32[]{:S(2)}, u32[]{:S(2)}) collective-permute-start(bf16[8,128,128]{2,1,0:T(8,128)(2,1)S(1)} %get-tuple-element.318), channel_id=1, source_target_pairs={{0,2},{2,4},{4,6},{6,8},{8,10},{10,12},{12,14},{14,16},{16,18},{18... | collective-permute-start | bytes 786440 | tf_op jit(solution)/shard_map/while/body/eval_jaxpr/ppermute | solution.py:12
  272.7 12.3 %collective-permute-start.1 = (bf16[8,128,128]{2,1,0:T(8,128)(2,1)S(1)}, bf16[8,128,128]{2,1,0:T(8,128)(2,1)S(1)}, u32[]{:S(2)}, u32[]{:S(2)}) collective-permute-start(bf16[8,128,128]{2,1,0:T(8,128)(2,1)S(1)} %get-tuple-element.318), channel_id=1, source_target_pairs={{0,2},{2,4},{4,6},{6,8},{8,10},{10,12},{12,14},{14,16},{16,18},{18... | collective-permute-start | bytes 786440 | tf_op jit(solution)/shard_map/while/body/eval_jaxpr/ppermute | solution.py:12
  285.9 12.5 %collective-permute-start.1 = (bf16[8,128,128]{2,1,0:T(8,128)(2,1)S(1)}, bf16[8,128,128]{2,1,0:T(8,128)(2,1)S(1)}, u32[]{:S(2)}, u32[]{:S(2)}) collective-permute-start(bf16[8,128,128]{2,1,0:T(8,128)(2,1)S(1)} %get-tuple-element.318), channel_id=1, source_target_pairs={{0,2},{2,4},{4,6},{6,8},{8,10},{10,12},{12,14},{14,16},{16,18},{18... | collective-permute-start | bytes 786440 | tf_op jit(solution)/shard_map/while/body/eval_jaxpr/ppermute | solution.py:12
  299.2 13.3 %collective-permute-start.1 = (bf16[8,128,128]{2,1,0:T(8,128)(2,1)S(1)}, bf16[8,128,128]{2,1,0:T(8,128)(2,1)S(1)}, u32[]{:S(2)}, u32[]{:S(2)}) collective-permute-start(bf16[8,128,128]{2,1,0:T(8,128)(2,1)S(1)} %get-tuple-element.318), channel_id=1, source_target_pairs={{0,2},{2,4},{4,6},{6,8},{8,10},{10,12},{12,14},{14,16},{16,18},{18... | collective-permute-start | bytes 786440 | tf_op jit(solution)/shard_map/while/body/eval_jaxpr/ppermute | solution.py:12
  303.3 6.2 %collective-permute-start = (bf16[]{:T(256)}, bf16[]{:T(256)}, u32[]{:S(2)}, u32[]{:S(2)}) collective-permute-start(bf16[]{:T(256)} %get-tuple-element.319), channel_id=1, source_target_pairs={{0,2},{2,4},{4,6},{6,8},{8,10},{10,12},{12,14},{14,16},{16,18},{18... | collective-permute-start | bytes 14 | tf_op jit(solution)/shard_map/while/body/eval_jaxpr/ppermute | solution.py:12
  313.2 13.5 %collective-permute-start.1 = (bf16[8,128,128]{2,1,0:T(8,128)(2,1)S(1)}, bf16[8,128,128]{2,1,0:T(8,128)(2,1)S(1)}, u32[]{:S(2)}, u32[]{:S(2)}) collective-permute-start(bf16[8,128,128]{2,1,0:T(8,128)(2,1)S(1)} %get-tuple-element.318), channel_id=1, source_target_pairs={{0,2},{2,4},{4,6},{6,8},{8,10},{10,12},{12,14},{14,16},{16,18},{18... | collective-permute-start | bytes 786440 | tf_op jit(solution)/shard_map/while/body/eval_jaxpr/ppermute | solution.py:12
  317.3 6.4 %collective-permute-start = (bf16[]{:T(256)}, bf16[]{:T(256)}, u32[]{:S(2)}, u32[]{:S(2)}) collective-permute-start(bf16[]{:T(256)} %get-tuple-element.319), channel_id=1, source_target_pairs={{0,2},{2,4},{4,6},{6,8},{8,10},{10,12},{12,14},{14,16},{16,18},{18... | collective-permute-start | bytes 14 | tf_op jit(solution)/shard_map/while/body/eval_jaxpr/ppermute | solution.py:12
  327.5 13.4 %collective-permute-start.1 = (bf16[8,128,128]{2,1,0:T(8,128)(2,1)S(1)}, bf16[8,128,128]{2,1,0:T(8,128)(2,1)S(1)}, u32[]{:S(2)}, u32[]{:S(2)}) collective-permute-start(bf16[8,128,128]{2,1,0:T(8,128)(2,1)S(1)} %get-tuple-element.318), channel_id=1, source_target_pairs={{0,2},{2,4},{4,6},{6,8},{8,10},{10,12},{12,14},{14,16},{16,18},{18... | collective-permute-start | bytes 786440 | tf_op jit(solution)/shard_map/while/body/eval_jaxpr/ppermute | solution.py:12
  331.6 6.3 %collective-permute-start = (bf16[]{:T(256)}, bf16[]{:T(256)}, u32[]{:S(2)}, u32[]{:S(2)}) collective-permute-start(bf16[]{:T(256)} %get-tuple-element.319), channel_id=1, source_target_pairs={{0,2},{2,4},{4,6},{6,8},{8,10},{10,12},{12,14},{14,16},{16,18},{18... | collective-permute-start | bytes 14 | tf_op jit(solution)/shard_map/while/body/eval_jaxpr/ppermute | solution.py:12
  341.7 13.1 %collective-permute-start.1 = (bf16[8,128,128]{2,1,0:T(8,128)(2,1)S(1)}, bf16[8,128,128]{2,1,0:T(8,128)(2,1)S(1)}, u32[]{:S(2)}, u32[]{:S(2)}) collective-permute-start(bf16[8,128,128]{2,1,0:T(8,128)(2,1)S(1)} %get-tuple-element.318), channel_id=1, source_target_pairs={{0,2},{2,4},{4,6},{6,8},{8,10},{10,12},{12,14},{14,16},{16,18},{18... | collective-permute-start | bytes 786440 | tf_op jit(solution)/shard_map/while/body/eval_jaxpr/ppermute | solution.py:12
  355.5 13.1 %collective-permute-start.1 = (bf16[8,128,128]{2,1,0:T(8,128)(2,1)S(1)}, bf16[8,128,128]{2,1,0:T(8,128)(2,1)S(1)}, u32[]{:S(2)}, u32[]{:S(2)}) collective-permute-start(bf16[8,128,128]{2,1,0:T(8,128)(2,1)S(1)} %get-tuple-element.318), channel_id=1, source_target_pairs={{0,2},{2,4},{4,6},{6,8},{8,10},{10,12},{12,14},{14,16},{16,18},{18... | collective-permute-start | bytes 786440 | tf_op jit(solution)/shard_map/while/body/eval_jaxpr/ppermute | solution.py:12
  369.4 13.1 %collective-permute-start.1 = (bf16[8,128,128]{2,1,0:T(8,128)(2,1)S(1)}, bf16[8,128,128]{2,1,0:T(8,128)(2,1)S(1)}, u32[]{:S(2)}, u32[]{:S(2)}) collective-permute-start(bf16[8,128,128]{2,1,0:T(8,128)(2,1)S(1)} %get-tuple-element.318), channel_id=1, source_target_pairs={{0,2},{2,4},{4,6},{6,8},{8,10},{10,12},{12,14},{14,16},{16,18},{18... | collective-permute-start | bytes 786440 | tf_op jit(solution)/shard_map/while/body/eval_jaxpr/ppermute | solution.py:12
  383.2 13.1 %collective-permute-start.1 = (bf16[8,128,128]{2,1,0:T(8,128)(2,1)S(1)}, bf16[8,128,128]{2,1,0:T(8,128)(2,1)S(1)}, u32[]{:S(2)}, u32[]{:S(2)}) collective-permute-start(bf16[8,128,128]{2,1,0:T(8,128)(2,1)S(1)} %get-tuple-element.318), channel_id=1, source_target_pairs={{0,2},{2,4},{4,6},{6,8},{8,10},{10,12},{12,14},{14,16},{16,18},{18... | collective-permute-start | bytes 786440 | tf_op jit(solution)/shard_map/while/body/eval_jaxpr/ppermute | solution.py:12
  397.1 13.1 %collective-permute-start.1 = (bf16[8,128,128]{2,1,0:T(8,128)(2,1)S(1)}, bf16[8,128,128]{2,1,0:T(8,128)(2,1)S(1)}, u32[]{:S(2)}, u32[]{:S(2)}) collective-permute-start(bf16[8,128,128]{2,1,0:T(8,128)(2,1)S(1)} %get-tuple-element.318), channel_id=1, source_target_pairs={{0,2},{2,4},{4,6},{6,8},{8,10},{10,12},{12,14},{14,16},{16,18},{18... | collective-permute-start | bytes 786440 | tf_op jit(solution)/shard_map/while/body/eval_jaxpr/ppermute | solution.py:12
  411.0 13.2 %collective-permute-start.1 = (bf16[8,128,128]{2,1,0:T(8,128)(2,1)S(1)}, bf16[8,128,128]{2,1,0:T(8,128)(2,1)S(1)}, u32[]{:S(2)}, u32[]{:S(2)}) collective-permute-start(bf16[8,128,128]{2,1,0:T(8,128)(2,1)S(1)} %get-tuple-element.318), channel_id=1, source_target_pairs={{0,2},{2,4},{4,6},{6,8},{8,10},{10,12},{12,14},{14,16},{16,18},{18... | collective-permute-start | bytes 786440 | tf_op jit(solution)/shard_map/while/body/eval_jaxpr/ppermute | solution.py:12
  415.1 6.0 collective-permute-start
  424.9 14.1 %collective-permute-start.1 = (bf16[8,128,128]{2,1,0:T(8,128)(2,1)S(1)}, bf16[8,128,128]{2,1,0:T(8,128)(2,1)S(1)}, u32[]{:S(2)}, u32[]{:S(2)}) collective-permute-start(bf16[8,128,128]{2,1,0:T(8,128)(2,1)S(1)} %get-tuple-element.318), channel_id=1, source_target_pairs={{0,2},{2,4},{4,6},{6,8},{8,10},{10,12},{12,14},{14,16},{16,18},{18... | collective-permute-start | bytes 786440 | tf_op jit(solution)/shard_map/while/body/eval_jaxpr/ppermute | solution.py:12
  429.4 6.6 %collective-permute-start = (bf16[]{:T(256)}, bf16[]{:T(256)}, u32[]{:S(2)}, u32[]{:S(2)}) collective-permute-start(bf16[]{:T(256)} %get-tuple-element.319), channel_id=1, source_target_pairs={{0,2},{2,4},{4,6},{6,8},{8,10},{10,12},{12,14},{14,16},{16,18},{18... | collective-permute-start | bytes 14 | tf_op jit(solution)/shard_map/while/body/eval_jaxpr/ppermute | solution.py:12
  439.8 14.9 %collective-permute-start.1 = (bf16[8,128,128]{2,1,0:T(8,128)(2,1)S(1)}, bf16[8,128,128]{2,1,0:T(8,128)(2,1)S(1)}, u32[]{:S(2)}, u32[]{:S(2)}) collective-permute-start(bf16[8,128,128]{2,1,0:T(8,128)(2,1)S(1)} %get-tuple-element.318), channel_id=1, source_target_pairs={{0,2},{2,4},{4,6},{6,8},{8,10},{10,12},{12,14},{14,16},{16,18},{18... | collective-permute-start | bytes 786440 | tf_op jit(solution)/shard_map/while/body/eval_jaxpr/ppermute | solution.py:12
  445.2 6.5 %collective-permute-start = (bf16[]{:T(256)}, bf16[]{:T(256)}, u32[]{:S(2)}, u32[]{:S(2)}) collective-permute-start(bf16[]{:T(256)} %get-tuple-element.319), channel_id=1, source_target_pairs={{0,2},{2,4},{4,6},{6,8},{8,10},{10,12},{12,14},{14,16},{16,18},{18... | collective-permute-start | bytes 14 | tf_op jit(solution)/shard_map/while/body/eval_jaxpr/ppermute | solution.py:12
  455.5 14.1 %collective-permute-start.1 = (bf16[8,128,128]{2,1,0:T(8,128)(2,1)S(1)}, bf16[8,128,128]{2,1,0:T(8,128)(2,1)S(1)}, u32[]{:S(2)}, u32[]{:S(2)}) collective-permute-start(bf16[8,128,128]{2,1,0:T(8,128)(2,1)S(1)} %get-tuple-element.318), channel_id=1, source_target_pairs={{0,2},{2,4},{4,6},{6,8},{8,10},{10,12},{12,14},{14,16},{16,18},{18... | collective-permute-start | bytes 786440 | tf_op jit(solution)/shard_map/while/body/eval_jaxpr/ppermute | solution.py:12
  460.0 6.5 %collective-permute-start = (bf16[]{:T(256)}, bf16[]{:T(256)}, u32[]{:S(2)}, u32[]{:S(2)}) collective-permute-start(bf16[]{:T(256)} %get-tuple-element.319), channel_id=1, source_target_pairs={{0,2},{2,4},{4,6},{6,8},{8,10},{10,12},{12,14},{14,16},{16,18},{18... | collective-permute-start | bytes 14 | tf_op jit(solution)/shard_map/while/body/eval_jaxpr/ppermute | solution.py:12
  (11 other events, 59.4 us)
Sparse Core Ops, SparseCore 0:
  8.9 16.3 all-gather.4
  28.0 197.1 all-gather.2
where the time goes:
time: 620 us; the launch traced here: 608 us
  waiting for transfers between devices  214 us (35%)
  starting transfers between devices  154 us (25%)
  local copies, waits for them, and re-layouts  115 us (19%)
  loops' own time  46.6 us (8%)
  matrix products  38.2 us (6%)
  other arithmetic  26 us (4%)
  between operations  14.6 us (2%)
    all_gather x1, waiting for transfers between devices, per_device(): lax.all_gather(w_qkv, 'ctx', axis=1, tiled=True)  200 us
    ppermute x30, starting transfers between devices, passed_along(): lax.ppermute(value, axis, [(source, source + steps) for source in range(l...  154 us
    dynamic_update_slice x4, local copies, waits for them, and re-layouts, complete(): lax.map(one_block, jnp.arange(row_count // block_rows, dtype=jnp.int32))  85 us
    another operation x1, loops' own time, per_device(): lax.fori_loop(0, lax.axis_size('ctx') - 1, hand_round, (own_pair, start_p...  45.3 us
    dot_general x1, matrix products, per_device(): jnp.einsum('tr,grc->gtc', whole, lax.all_gather(w_qkv, 'ctx', axis=1, til...  17.1 us
    dot_general x2, matrix products, one_block(): jnp.einsum('hbs,she->bhe', weights, values, preferred_element_type=jnp.fl...  16.2 us
    all_gather x1, waiting for transfers between devices, per_device(): whole = lax.all_gather(tokens, 'head', axis=1, tiled=True)  13.4 us
  transfers between devices with their start and end apart: 32, of which 2 were waited for; matrix products, arithmetic and copies ran while one was open for 1% of the time, Pallas kernels for 0%

commit v1 on v0

v1 whole, which is shorter than its diff:
```python
import functools

import jax
import jax.numpy as jnp
from jax import lax
from jax.experimental import pallas as pl
from jax.experimental.pallas import tpu as pltpu
from jax.sharding import PartitionSpec as P

HEAD_DIM = 128
CHUNK = 256
MESH = pl.DeviceIdType.MESH
F32, BF16 = jnp.float32, jnp.bfloat16
GROUPS = ((1, 0), (2, 0), (1, 1), (2, 1), (0, 0), (0, 1))


def dot(left, right, dims=((1,), (0,))):
    return lax.dot_general(left, right, (dims, ((), ())), preferred_element_type=F32)


def kernel(
    n, nh, tok_ref, w_ref, gain_ref, row_ref, col_ref, out_ref,
    wbuf, tok, qkv, local, incoming, state_out, state_got, tail_out, tail_got,
    z_send, z_recv, f_send, f_recv, s_send, s_recv,
    tok_send, tok_recv, tok_own, st_send, st_recv, tl_send, tl_recv,
):
    lines = n // 4
    span = n // 4
    rows, width = tok_ref.shape[0], tok_ref.shape[1]
    cols = wbuf.shape[-1]
    depth = n * wbuf.shape[-2]
    heads = cols // HEAD_DIM
    chunks = rows // CHUNK
    ctx, head = lax.axis_index("ctx"), lax.axis_index("head")
    a, b, c = ctx // 4, (ctx // 2) % 2, ctx % 2

    def place(a_, b_, c_):
        return (a_ * 4 + b_ * 2 + c_, head)

    def line_at(step):
        return lax.rem(a - step + lines, lines)

    def flip(flag, yes):
        return 1 - flag if yes else flag

    for g, (which, half) in enumerate(GROUPS):
        wbuf[g, a, b, c] = w_ref[which, :, half * cols:(half + 1) * cols]
    own_tail = jnp.max(row_ref[...], axis=1, keepdims=True)
    tail_out[...] = jnp.broadcast_to(own_tail, tail_out.shape)

    barrier = pltpu.get_barrier_semaphore()

    def greet(where):
        pl.semaphore_signal(barrier, inc=1, device_id=where, device_id_type=MESH)

    greet(place(a, b, 1 - c))
    greet(place(a, 1 - b, c))

    @pl.loop(1, lines)
    def _(d):
        greet(place(lax.rem(a + d, lines), b, c))

    @pl.loop(1, span + 1)
    def _(d):
        greet((lax.rem(ctx + d, n), head))
        greet((lax.rem(ctx - d + n, n), head))

    @pl.loop(1, nh)
    def _(d):
        greet((ctx, lax.rem(head + d, nh)))

    pl.semaphore_wait(barrier, 2 + (lines - 1) + 2 * span + (nh - 1))

    def remote(src, dst, send, recv, where):
        return pltpu.make_async_remote_copy(
            src_ref=src, dst_ref=dst, send_sem=send, recv_sem=recv,
            device_id=where, device_id_type=MESH,
        )

    def z_copy(g, d, slot_line, to_line):
        slot = wbuf.at[g, slot_line, b, c]
        return remote(slot, slot, z_send.at[g, d - 1], z_recv.at[g, d - 1], place(to_line, b, c))

    def f_copy(g, k, got):
        odd = g % 2
        slot = wbuf.at[g, line_at(k), flip(b, got and odd), flip(c, got and not odd)]
        where = place(a, flip(b, odd), flip(c, not odd))
        return remote(slot, slot, f_send.at[g, k], f_recv.at[g, k], where)

    def s_copy(g, k, far, got):
        odd = g % 2
        b_, c_ = (flip(b, far), flip(c, got)) if odd else (flip(b, got), flip(c, far))
        slot = wbuf.at[g, line_at(k), b_, c_]
        where = place(a, flip(b, not odd), flip(c, odd))
        at = k + (lines if far else 0)
        return remote(slot, slot, s_send.at[g, at], s_recv.at[g, at], where)

    def tok_copy(d, from_head, to_head):
        there = tok.at[:, pl.ds(pl.multiple_of(from_head * width, 128), width)]
        return remote(tok_ref, there, tok_send.at[d - 1], tok_recv.at[d - 1], (ctx, to_head))

    def state_copy(half, j):
        part = pl.ds(half * heads, heads)
        return remote(
            state_out.at[part], state_got.at[j, part], st_send.at[half, j], st_recv.at[half, j],
            (lax.rem(ctx + j + 1, n), head),
        )

    def tail_copy(j):
        return remote(
            tail_out, tail_got.at[j], tl_send.at[j], tl_recv.at[j], (lax.rem(ctx + j + 1, n), head)
        )

    def begin(pair):
        for g in pair:
            f_copy(g, 0, False).start()
            s_copy(g, 0, False, False).start()

        @pl.loop(1, lines)
        def _(d):
            for g in pair:
                z_copy(g, d, a, lax.rem(a + d, lines)).start()

    def pass_lines(pair):
        @pl.loop(1, lines)
        def _(d):
            for g in pair:
                z_copy(g, d, line_at(d), a).wait_recv()
                f_copy(g, d, False).start()
                s_copy(g, d, False, False).start()

    def pass_first(pair):
        @pl.loop(0, lines)
        def _(d):
            for g in pair:
                f_copy(g, d, True).wait_recv()
                s_copy(g, d, True, False).start()

    def finish(g):
        @pl.loop(0, lines)
        def _(d):
            s_copy(g, d, False, True).wait_recv()
            s_copy(g, d, True, True).wait_recv()

    def project(g):
        which, half = GROUPS[g]

        @pl.loop(0, chunks)
        def _(i):
            part = pl.ds(pl.multiple_of(i * CHUNK, CHUNK), CHUNK)
            weights = wbuf[g].reshape(depth, cols)
            got = dot(tok[part, :], weights).astype(BF16)
            if which < 2:
                wide = got.astype(F32)
                got = jnp.where(wide > 0.0, wide + 1.0, jnp.exp(jnp.minimum(wide, 0.0))).astype(BF16)
            qkv[which, part, half * cols:(half + 1) * cols] = got

    def own_states(half):
        for h in range(heads):
            at = half * heads + h
            lanes = pl.ds(at * HEAD_DIM, HEAD_DIM)
            state = jnp.zeros((HEAD_DIM, HEAD_DIM), F32)
            before = None
            for i in range(chunks):
                part = pl.ds(i * CHUNK, CHUNK)
                ids = row_ref[:, part]
                first = jnp.min(ids, axis=1, keepdims=True)
                tail = jnp.max(ids, axis=1, keepdims=True)
                if i > 0:
                    state = jnp.where(before == first, state, 0.0)
                local[i, at] = state
                keys = qkv[1, part, lanes]
                keys = jnp.where(col_ref[part, :] == tail, keys, jnp.zeros_like(keys))
                fresh = dot(keys, qkv[2, part, lanes], ((0,), (0,)))
                state = jnp.where(first == tail, state, 0.0) + fresh
                before = tail
            state_out[at] = state.astype(BF16)

        @pl.loop(0, span)
        def _(j):
            state_copy(half, j).start()

    def add_states():
        first = jnp.min(row_ref[:, pl.ds(0, CHUNK)], axis=1, keepdims=True)
        incoming[...] = jnp.zeros_like(incoming)

        @pl.loop(0, span)
        def _(j):
            tail_copy(j).wait_recv()
            for half in range(2):
                state_copy(half, j).wait_recv()
            ids = tail_got[j][0:1, :] + jnp.where(ctx > j, 0, -1000)
            linked = ids == first
            for at in range(2 * heads):
                incoming[at] += jnp.where(linked, state_got[j, at].astype(F32), 0.0)

        for i in range(chunks):
            ids = row_ref[:, pl.ds(i * CHUNK, CHUNK)]
            here = jnp.min(ids, axis=1, keepdims=True)
            for at in range(2 * heads):
                local[i, at] += jnp.where(here == first, incoming[at], 0.0)

    def attend(half):
        @pl.loop(0, chunks)
        def _(i):
            part = pl.ds(pl.multiple_of(i * CHUNK, CHUNK), CHUNK)
            ids_row, ids_col = row_ref[:, part], col_ref[part, :]
            first = jnp.min(ids_row, axis=1, keepdims=True)
            later = lax.broadcasted_iota(jnp.int32, (CHUNK, CHUNK), 0)
            sooner = lax.broadcasted_iota(jnp.int32, (CHUNK, CHUNK), 1)
            visible = (sooner <= later) & (ids_row == ids_col)
            reached = ids_col == first
            for h in range(heads):
                at = half * heads + h
                lanes = pl.ds(at * HEAD_DIM, HEAD_DIM)
                query = qkv[0, part, lanes]
                scores = dot(query, qkv[1, part, lanes], ((1,), (1,)))
                scores = jnp.where(visible, scores, 0.0).astype(BF16)
                total = dot(scores, qkv[2, part, lanes])
                prefix = dot(query, local[i, at].astype(BF16))
                total = total + jnp.where(reached, prefix, 0.0)
                scale = lax.rsqrt(jnp.mean(total * total, axis=1, keepdims=True) + 1e-05)
                out_ref[part, lanes] = (total * scale * gain_ref[:, lanes]).astype(BF16)

    pairs = ((0, 1), (2, 3), (4, 5))
    begin(pairs[0])

    @pl.loop(1, nh)
    def _(d):
        tok_copy(d, head, lax.rem(head + d, nh)).start()

    own = pltpu.make_async_copy(
        tok_ref, tok.at[:, pl.ds(pl.multiple_of(head * width, 128), width)], tok_own
    )
    own.start()

    @pl.loop(0, span)
    def _(j):
        tail_copy(j).start()

    begin(pairs[1])
    pass_lines(pairs[0])
    pass_first(pairs[0])
    own.wait()

    @pl.loop(1, nh)
    def _(d):
        tok_copy(d, lax.rem(head - d + nh, nh), head).wait_recv()

    pass_lines(pairs[1])
    for g in pairs[0]:
        finish(g)
        project(g)
    begin(pairs[2])
    own_states(0)
    pass_first(pairs[1])
    pass_lines(pairs[2])
    for g in pairs[1]:
        finish(g)
        project(g)
    own_states(1)
    pass_first(pairs[2])
    add_states()
    for g in pairs[2]:
        finish(g)
        project(g)
        attend(GROUPS[g][1])

    @pl.loop(1, lines)
    def _(d):
        for g in range(len(GROUPS)):
            z_copy(g, d, a, lax.rem(a + d, lines)).wait_send()

    @pl.loop(0, lines)
    def _(d):
        for g in range(len(GROUPS)):
            f_copy(g, d, False).wait_send()
            s_copy(g, d, False, False).wait_send()
            s_copy(g, d, True, False).wait_send()

    @pl.loop(1, nh)
    def _(d):
        tok_copy(d, head, lax.rem(head + d, nh)).wait_send()

    @pl.loop(0, span)
    def _(j):
        tail_copy(j).wait_send()
        for half in range(2):
            state_copy(half, j).wait_send()


def per_device(n, nh, tokens, w_qkv, out_gain, seg_ids):
    rows, width = tokens.shape
    part_rows, own_cols = w_qkv.shape[1:]
    cols = own_cols // 2
    heads = own_cols // HEAD_DIM
    lines = span = n // 4
    groups = len(GROUPS)
    vmem = pl.BlockSpec(memory_space=pltpu.VMEM)
    dma = pltpu.SemaphoreType.DMA
    state = (heads, HEAD_DIM, HEAD_DIM)
    return pl.pallas_call(
        functools.partial(kernel, n, nh),
        out_shape=jax.ShapeDtypeStruct((rows, own_cols), BF16),
        in_specs=[pl.BlockSpec(memory_space=pl.ANY), vmem, vmem, vmem, vmem],
        out_specs=vmem,
        scratch_shapes=[
            pltpu.VMEM((groups, lines, 2, 2, part_rows, cols), BF16),
            pltpu.VMEM((rows, width * nh), BF16),
            pltpu.VMEM((3, rows, own_cols), BF16),
            pltpu.VMEM((rows // CHUNK,) + state, F32),
            pltpu.VMEM(state, F32),
            pltpu.VMEM(state, BF16),
            pltpu.VMEM((span,) + state, BF16),
            pltpu.VMEM((8, HEAD_DIM), jnp.int32),
            pltpu.VMEM((span, 8, HEAD_DIM), jnp.int32),
            dma((groups, lines - 1)), dma((groups, lines - 1)),
            dma((groups, lines)), dma((groups, lines)),
            dma((groups, 2 * lines)), dma((groups, 2 * lines)),
            dma((nh - 1,)), dma((nh - 1,)), dma,
            dma((2, span)), dma((2, span)),
            dma((span,)), dma((span,)),
        ],
        compiler_params=pltpu.CompilerParams(
            collective_id=0, has_side_effects=True, vmem_limit_bytes=56 * 1024 * 1024
        ),
        cost_estimate=pl.CostEstimate(
            flops=2 * rows * width * nh * own_cols * 3,
            bytes_accessed=4 * rows * width, transcendentals=rows * own_cols,
        ),
    )(
        tokens, w_qkv, out_gain.reshape(1, own_cols),
        seg_ids.reshape(1, rows), seg_ids.reshape(rows, 1),
    )


def solution(mesh):
    placed = (P("ctx", "head"), P(None, "ctx", "head"), P("head"), P("ctx"))
    sizes = (mesh.shape["ctx"], mesh.shape["head"])
    return jax.shard_map(
        functools.partial(per_device, *sizes),
        mesh=mesh, in_specs=placed, out_specs=P("ctx", "head"), check_vma=False,
    )
```

time: 620 us -> 150 us (0.24)
  the two profiles are of different devices: /device:TPU:0 before, /device:TPU:8 now
where the time goes in v1:
time: 150 us
  Pallas kernels  145 us (97%)
  local copies, waits for them, and re-layouts  4.79 us (3%)
    pallas_call x1, Pallas kernels, per_device(): pl.pallas_call(functools.partial(kernel, n, nh), out_shape=jax.ShapeDtype...  145 us
    unnamed x1, local copies, waits for them, and re-layouts  3.08 us

profile of v1, /device:TPU:8, one launch (start us, length us, event | category | flops | bytes accessed | tf_op | source)
XLA Modules:
  0.0 150.1 jit_solution(16648520704876117825)
XLA Ops:
  0.0 1.7 %copy.5.col_ref = s32[1024,1]{1,0:T(8,128)} copy(s32[1024,1]{0,1:T(1,128)} %bitcast.3) | data formatting | bytes 8192 | tf_op jit(solution)/shard_map/reshape | solution.py:333
  1.7 145.3 %shard_map.46 = bf16[1024,1024]{1,0:T(8,128)(2,1)} custom-call(bf16[1024,1024]{1,0:T(8,128)(2,1)} %tok_ref.1, bf16[3,128,1024]{2,1,0:T(8,128)(2,1)} %w_ref.1, f32[1,1024]{1,0:T(1,128)} %bitcast.5, s32[1,1024]{1,0:T(1,128)} %bitcast.4, s32[1024,1]{1,0:T(8,128)} %copy.5.col_ref), custom_call_target="tpu_custom_call" | custom-call | flops 12884901888 | bytes 4194304 | tf_op jit(solution)/shard_map/pallas_call | solution.py:302
  147.0 3.1 %copy.7 = bf16[1024,1024]{1,0:T(8,128)(2,1)} copy(bf16[1024,1024]{1,0:T(8,128)(2,1)} %shard_map.46) | data formatting | bytes 4194304

commit v2 on v1

v2 whole, which is shorter than its diff:
```python
import functools

import jax
import jax.numpy as jnp
from jax import lax
from jax.experimental import pallas as pl
from jax.experimental.pallas import tpu as pltpu
from jax.sharding import PartitionSpec as P

HEAD_DIM = 128
CHUNK = 256
MESH = pl.DeviceIdType.MESH
F32, BF16 = jnp.float32, jnp.bfloat16


def groups_of(halves):
    keys_values = tuple((which, half) for half in range(halves) for which in (1, 2))
    return keys_values + tuple((0, half) for half in range(halves))


def dot(left, right, dims=((1,), (0,))):
    return lax.dot_general(left, right, (dims, ((), ())), preferred_element_type=F32)


def kernel(
    n, nh, halves, tok_ref, w_ref, gain_ref, row_ref, out_ref,
    wbuf, wout, tok, qkv, outs, local, incoming, state_out, state_got, row, col, tail_out, tail_got,
    x_send, x_recv, z_send, z_recv, y_send, y_recv,
    tok_send, tok_recv, tok_own, px_send, px_recv, ph_send, ph_recv,
    st_send, st_recv, tl_send, tl_recv, row_send, row_recv, out_send, out_recv, out_own,
):
    lines = n // 4
    pairs = n // 2
    span = n // 8
    rows, width = tok_ref.shape[0], tok_ref.shape[1]
    cols = wbuf.shape[-1]
    depth = n * wbuf.shape[-2]
    heads = cols // HEAD_DIM
    chunks = rows // CHUNK
    groups = groups_of(halves)
    last = len(groups) - 1
    ctx, head = lax.axis_index("ctx"), lax.axis_index("head")
    a, b, c = ctx // 4, (ctx // 2) % 2, ctx % 2
    pair = ctx // 2

    def place(a_, b_, c_):
        return (a_ * 4 + b_ * 2 + c_, head)

    def line_at(step):
        return lax.rem(a - step + lines, lines)

    for g, (which, half) in enumerate(groups):
        keep = pl.ds(pl.multiple_of((c * halves + half) * cols, 128), cols)
        give = pl.ds(pl.multiple_of(((1 - c) * halves + half) * cols, 128), cols)
        wbuf[g, a, b, c] = w_ref[which, :, keep]
        wout[g] = w_ref[which, :, give]
    row[c] = row_ref[...]

    barrier = pltpu.get_barrier_semaphore()

    def greet(where):
        pl.semaphore_signal(barrier, inc=1, device_id=where, device_id_type=MESH)

    greet(place(a, b, 1 - c))
    greet(place(a, 1 - b, c))

    @pl.loop(1, lines)
    def _(d):
        greet(place(lax.rem(a + d, lines), b, c))

    @pl.loop(1, span + 1)
    def _(d):
        greet((lax.rem(pair + d, pairs) * 2 + c, head))
        greet((lax.rem(pair - d + pairs, pairs) * 2 + c, head))

    @pl.loop(1, nh)
    def _(d):
        greet((ctx, lax.rem(head + d, nh)))

    pl.semaphore_wait(barrier, 2 + (lines - 1) + 2 * span + (nh - 1))

    def remote(src, dst, send, recv, where):
        return pltpu.make_async_remote_copy(
            src_ref=src, dst_ref=dst, send_sem=send, recv_sem=recv,
            device_id=where, device_id_type=MESH,
        )

    def x_copy(g, c_):
        return remote(
            wout.at[g], wbuf.at[g, a, b, c_], x_send.at[g], x_recv.at[g], place(a, b, 1 - c)
        )

    def z_copy(g, d, far, slot_line, to_line):
        slot = wbuf.at[g, slot_line, b, 1 - c if far else c]
        at = d - 1 + (lines - 1 if far else 0)
        return remote(slot, slot, z_send.at[g, at], z_recv.at[g, at], place(to_line, b, c))

    def y_copy(g, k, far, b_):
        slot = wbuf.at[g, line_at(k), b_, 1 - c if far else c]
        at = k + (lines if far else 0)
        return remote(slot, slot, y_send.at[g, at], y_recv.at[g, at], place(a, 1 - b, c))

    def features(of):
        return pl.ds(pl.multiple_of(of * width, 128), width)

    def own_rows(of):
        return pl.ds(pl.multiple_of(of * rows, CHUNK), rows)

    def piece(of, i):
        return pl.ds(pl.multiple_of(of * rows + i * CHUNK, CHUNK), CHUNK)

    def tok_copy(d, of, to):
        there = tok.at[own_rows(c), features(of)]
        return remote(tok_ref, there, tok_send.at[d - 1], tok_recv.at[d - 1], (ctx, to))

    def px_copy(i, of):
        return remote(
            tok_ref.at[pl.ds(i * CHUNK, CHUNK)], tok.at[piece(of, i), features(head)],
            px_send.at[i], px_recv.at[i], place(a, b, 1 - c),
        )

    def ph_copy(i, d, of, to):
        there = tok.at[piece(1 - c, i), features(of)]
        return remote(there, there, ph_send.at[i, d - 1], ph_recv.at[i, d - 1], (ctx, to))

    def state_copy(half, j):
        part = pl.ds(half * heads, heads)
        return remote(
            state_out.at[part], state_got.at[j, part], st_send.at[half, j], st_recv.at[half, j],
            (lax.rem(pair + j + 1, pairs) * 2 + c, head),
        )

    def tail_copy(j):
        return remote(
            tail_out, tail_got.at[j], tl_send.at[j], tl_recv.at[j],
            (lax.rem(pair + j + 1, pairs) * 2 + c, head),
        )

    def row_copy(c_):
        return remote(row.at[c_], row.at[c_], row_send, row_recv, place(a, b, 1 - c))

    def out_copy(half, i, of):
        part = pl.ds(half * cols, cols)
        there = pl.ds(pl.multiple_of((of * halves + half) * cols, 128), cols)
        at = pl.ds(pl.multiple_of(i * CHUNK, CHUNK), CHUNK)
        return remote(
            outs.at[piece(1 - c, i), part], out_ref.at[at, there],
            out_send.at[half, i], out_recv.at[half, i], place(a, b, 1 - c),
        )

    def out_keep(half):
        there = pl.ds(pl.multiple_of((c * halves + half) * cols, 128), cols)
        return pltpu.make_async_copy(
            outs.at[own_rows(c), pl.ds(half * cols, cols)], out_ref.at[:, there], out_own.at[half]
        )

    def next_head(d):
        return lax.rem(head + d, nh)

    def prior_head(d):
        return lax.rem(head - d + nh, nh)

    def spread(g, far):
        y_copy(g, 0, far, b).start()

        @pl.loop(1, lines)
        def _(d):
            z_copy(g, d, far, a, lax.rem(a + d, lines)).start()

    def begin(g):
        x_copy(g, c).start()
        spread(g, False)

    def pass_partner(g):
        x_copy(g, 1 - c).wait_recv()
        spread(g, True)

    def pass_lines(g):
        @pl.loop(1, lines)
        def _(d):
            for far in (False, True):
                z_copy(g, d, far, line_at(d), a).wait_recv()
                y_copy(g, d, far, b).start()

    def finish(g):
        @pl.loop(0, lines)
        def _(d):
            for far in (False, True):
                y_copy(g, d, far, 1 - b).wait_recv()

    def project(g, of, i, height):
        which, half = groups[g]
        part = pl.ds(pl.multiple_of(of * rows + i * height, height), height)
        got = dot(tok[part, :], wbuf[g].reshape(depth, cols)).astype(BF16)
        if which < 2:
            wide = got.astype(F32)
            got = jnp.where(wide > 0.0, wide + 1.0, jnp.exp(jnp.minimum(wide, 0.0))).astype(BF16)
        qkv[which, part, half * cols:(half + 1) * cols] = got

    def project_own(g):
        @pl.loop(0, rows // 512)
        def _(i):
            project(g, c, i, 512)

    def ids_of(i):
        return row[i // chunks, :, (i % chunks) * CHUNK:(i % chunks + 1) * CHUNK]

    def least(ids):
        return jnp.min(ids, axis=1, keepdims=True)

    def most(ids):
        return jnp.max(ids, axis=1, keepdims=True)

    def own_states(half):
        for h in range(heads):
            at = half * heads + h
            lanes = pl.ds(at * HEAD_DIM, HEAD_DIM)
            state = jnp.zeros((HEAD_DIM, HEAD_DIM), F32)
            before = None
            for i in range(2 * chunks):
                part = pl.ds(i * CHUNK, CHUNK)
                first, tail = least(ids_of(i)), most(ids_of(i))
                if i > 0:
                    state = jnp.where(before == first, state, 0.0)
                local[i, at] = state
                keys = qkv[1, part, lanes]
                keys = jnp.where(col[part, 0:1] == tail, keys, jnp.zeros_like(keys))
                fresh = dot(keys, qkv[2, part, lanes], ((0,), (0,)))
                state = jnp.where(first == tail, state, 0.0) + fresh
                before = tail
            state_out[at] = state.astype(BF16)

        @pl.loop(0, span)
        def _(j):
            state_copy(half, j).start()

    def add_states():
        first = least(ids_of(0))
        incoming[...] = jnp.zeros_like(incoming)

        @pl.loop(0, span)
        def _(j):
            tail_copy(j).wait_recv()
            for half in range(halves):
                state_copy(half, j).wait_recv()
            ids = tail_got[j][0:1, :] + jnp.where(pair > j, 0, -1000)
            linked = ids == first
            for at in range(halves * heads):
                incoming[at] += jnp.where(linked, state_got[j, at].astype(F32), 0.0)

        for i in range(2 * chunks):
            here = least(ids_of(i))
            for at in range(halves * heads):
                local[i, at] += jnp.where(here == first, incoming[at], 0.0)

    def attend(half, of, i):
        part = piece(of, i)
        ids_row = row[of, :, pl.ds(pl.multiple_of(i * CHUNK, CHUNK), CHUNK)]
        ids_col = col[part, 0:1]
        later = lax.broadcasted_iota(jnp.int32, (CHUNK, CHUNK), 0)
        sooner = lax.broadcasted_iota(jnp.int32, (CHUNK, CHUNK), 1)
        visible = (sooner <= later) & (ids_row == ids_col)
        reached = ids_col == least(ids_row)
        for h in range(heads):
            at = half * heads + h
            lanes = pl.ds(at * HEAD_DIM, HEAD_DIM)
            query = qkv[0, part, lanes]
            scores = dot(query, qkv[1, part, lanes], ((1,), (1,)))
            scores = jnp.where(visible, scores, 0.0).astype(BF16)
            total = dot(scores, qkv[2, part, lanes])
            prefix = dot(query, local[of * chunks + i, at].astype(BF16))
            total = total + jnp.where(reached, prefix, 0.0)
            scale = lax.rsqrt(jnp.mean(total * total, axis=1, keepdims=True) + 1e-05)
            gain = gain_ref[:, pl.ds(pl.multiple_of((c * halves * heads + at) * HEAD_DIM, 128), HEAD_DIM)]
            outs[part, lanes] = (total * scale * gain).astype(BF16)

    def attend_all(half):
        @pl.loop(0, chunks)
        def _(i):
            attend(half, 1 - c, i)
            out_copy(half, i, c).start()

        @pl.loop(0, chunks)
        def _(i):
            attend(half, c, i)

        out_keep(half).start()

    begin(0)
    row_copy(c).start()

    @pl.loop(1, nh)
    def _(d):
        tok_copy(d, head, next_head(d)).start()

    own = pltpu.make_async_copy(tok_ref, tok.at[own_rows(c), features(head)], tok_own)
    own.start()
    begin(1)
    begin(2)
    px_copy(0, c).start()
    pass_partner(0)
    pass_partner(1)
    row_copy(1 - c).wait_recv()
    tail_out[...] = jnp.broadcast_to(most(row[1]), tail_out.shape)

    @pl.loop(0, span)
    def _(j):
        tail_copy(j).start()

    for i in range(2 * chunks):
        col[pl.ds(i * CHUNK, CHUNK), :] = jnp.broadcast_to(ids_of(i), (HEAD_DIM, CHUNK)).T
    pass_lines(0)

    for g in range(last + 1):
        if g + 3 <= last:
            begin(g + 3)
        if g <= last - 2:
            for i in range(g + 1, chunks if g == last - 2 else min(g + 2, chunks)):
                px_copy(i, c).start()
        if g + 2 <= last:
            pass_partner(g + 2)
        if g + 1 <= last:
            pass_lines(g + 1)
        if g == 0:
            own.wait()

            @pl.loop(1, nh)
            def _(d):
                tok_copy(d, prior_head(d), head).wait_recv()

        if g == last:
            ready, fresh = chunks, ()
        else:
            ready = min(max(g - 1, 0), chunks)
            fresh = range(ready, chunks if g == last - 1 else min(g, chunks))
        for i in fresh:
            px_copy(i, 1 - c).wait_recv()

            @pl.loop(1, nh)
            def _(d):
                ph_copy(i, d, head, next_head(d)).start()

        finish(g)
        project_own(g)
        if ready > 0:
            @pl.loop(0, ready)
            def _(i):
                project(g, 1 - c, i, CHUNK)

        for i in fresh:
            @pl.loop(1, nh)
            def _(d):
                ph_copy(i, d, prior_head(d), head).wait_recv()

            for earlier in range(g + 1):
                project(earlier, 1 - c, i, CHUNK)
        if g == last - 1:
            for half in range(halves):
                own_states(half)
            add_states()
            for half in range(halves - 1):
                attend_all(half)
    attend_all(halves - 1)

    for g in range(last + 1):
        x_copy(g, c).wait_send()

        @pl.loop(1, lines)
        def _(d):
            for far in (False, True):
                z_copy(g, d, far, a, lax.rem(a + d, lines)).wait_send()

        @pl.loop(0, lines)
        def _(d):
            for far in (False, True):
                y_copy(g, d, far, b).wait_send()

    row_copy(c).wait_send()

    @pl.loop(1, nh)
    def _(d):
        tok_copy(d, head, next_head(d)).wait_send()

    for i in range(chunks):
        px_copy(i, c).wait_send()

        @pl.loop(1, nh)
        def _(d):
            ph_copy(i, d, head, next_head(d)).wait_send()

    @pl.loop(0, span)
    def _(j):
        tail_copy(j).wait_send()
        for half in range(halves):
            state_copy(half, j).wait_send()

    for half in range(halves):
        out_keep(half).wait()

        @pl.loop(0, chunks)
        def _(i):
            out_copy(half, i, c).wait_send()
            out_copy(half, i, 1 - c).wait_recv()


def per_device(n, nh, tokens, w_qkv, out_gain, seg_ids):
    rows, width = tokens.shape
    part_rows, own_cols = w_qkv.shape[1:]
    halves = 2 if own_cols >= 4 * HEAD_DIM else 1
    cols = own_cols // (2 * halves)
    heads = own_cols // 2 // HEAD_DIM
    lines, span, chunks = n // 4, n // 8, rows // CHUNK
    groups = 3 * halves
    vmem = pl.BlockSpec(memory_space=pltpu.VMEM)
    hbm = pl.BlockSpec(memory_space=pl.ANY)
    dma = pltpu.SemaphoreType.DMA
    state = (heads, HEAD_DIM, HEAD_DIM)
    return pl.pallas_call(
        functools.partial(kernel, n, nh, halves),
        out_shape=jax.ShapeDtypeStruct((rows, own_cols), BF16),
        in_specs=[hbm, vmem, vmem, vmem],
        out_specs=hbm,
        scratch_shapes=[
            pltpu.VMEM((groups, lines, 2, 2, part_rows, cols), BF16),
            pltpu.VMEM((groups, part_rows, cols), BF16),
            pltpu.VMEM((2 * rows, width * nh), BF16),
            pltpu.VMEM((3, 2 * rows, halves * cols), BF16),
            pltpu.VMEM((2 * rows, halves * cols), BF16),
            pltpu.VMEM((2 * chunks,) + state, F32),
            pltpu.VMEM(state, F32),
            pltpu.VMEM(state, BF16),
            pltpu.VMEM((span,) + state, BF16),
            pltpu.VMEM((2, 1, rows), jnp.int32),
            pltpu.VMEM((2 * rows, HEAD_DIM), jnp.int32),
            pltpu.VMEM((8, HEAD_DIM), jnp.int32),
            pltpu.VMEM((span, 8, HEAD_DIM), jnp.int32),
            dma((groups,)), dma((groups,)),
            dma((groups, 2 * lines - 2)), dma((groups, 2 * lines - 2)),
            dma((groups, 2 * lines)), dma((groups, 2 * lines)),
            dma((nh - 1,)), dma((nh - 1,)), dma,
            dma((chunks,)), dma((chunks,)),
            dma((chunks, nh - 1)), dma((chunks, nh - 1)),
            dma((halves, span)), dma((halves, span)),
            dma((span,)), dma((span,)),
            dma, dma,
            dma((halves, chunks)), dma((halves, chunks)), dma((halves,)),
        ],
        compiler_params=pltpu.CompilerParams(
            collective_id=0, has_side_effects=True, vmem_limit_bytes=56 * 1024 * 1024
        ),
        cost_estimate=pl.CostEstimate(
            flops=2 * rows * width * nh * own_cols * 3,
            bytes_accessed=4 * rows * width, transcendentals=rows * own_cols,
        ),
    )(tokens, w_qkv, out_gain.reshape(1, own_cols), seg_ids.reshape(1, rows))


def solution(mesh):
    placed = (P("ctx", "head"), P(None, "ctx", "head"), P("head"), P("ctx"))
    sizes = (mesh.shape["ctx"], mesh.shape["head"])
    return jax.shard_map(
        functools.partial(per_device, *sizes),
        mesh=mesh, in_specs=placed, out_specs=P("ctx", "head"), check_vma=False,
    )
```

time: 150 us -> 124 us (0.83)
  the two profiles are of different devices: /device:TPU:8 before, /device:TPU:0 now
where the time goes in v2:
time: 124 us
  Pallas kernels  121 us (98%)
  local copies, waits for them, and re-layouts  3.08 us (2%)
    pallas_call x1, Pallas kernels, per_device(): pl.pallas_call(functools.partial(kernel, n, nh, halves), out_shape=jax.Sh...  121 us
    unnamed x1, local copies, waits for them, and re-layouts  3.08 us

profile of v2, /device:TPU:0, one launch (start us, length us, event | category | flops | bytes accessed | tf_op | source)
XLA Modules:
  0.0 124.1 jit_solution(17074398022113050066)
XLA Ops:
  0.0 121.0 %shard_map.46 = bf16[1024,1024]{1,0:T(8,128)(2,1)} custom-call(bf16[1024,1024]{1,0:T(8,128)(2,1)} %tok_ref.1, bf16[3,128,1024]{2,1,0:T(8,128)(2,1)} %w_ref.1, f32[1,1024]{1,0:T(1,128)} %bitcast.2, s32[1,1024]{1,0:T(1,128)} %bitcast.3), custom_call_target="tpu_custom_call" | custom-call | flops 12884901888 | bytes 4194304 | tf_op jit(solution)/shard_map/pallas_call | solution.py:418
  121.0 3.1 %copy.6 = bf16[1024,1024]{1,0:T(8,128)(2,1)} copy(bf16[1024,1024]{1,0:T(8,128)(2,1)} %shard_map.46) | data formatting | bytes 4194304

commit v3 on v2

--- a/solution.py
+++ b/solution.py
@@ -13,9 +13,13 @@
 F32, BF16 = jnp.float32, jnp.bfloat16
 
 
-def groups_of(halves):
-    keys_values = tuple((which, half) for half in range(halves) for which in (1, 2))
-    return keys_values + tuple((0, half) for half in range(halves))
+def groups_of(heads):
+    if heads % 4:
+        return ((1, 0, heads), (2, 0, heads), (0, 0, heads))
+    half = heads // 2
+    first = tuple((which, 0, half) for which in (1, 2, 0))
+    second = tuple((which, half, half) for which in (1, 2))
+    return first + second + ((0, half, half // 2), (0, half + half // 2, half // 2))
 
 
 def dot(left, right, dims=((1,), (0,))):
@@ -23,8 +27,7 @@
 
 
 def kernel(
-    n, nh, halves, tok_ref, w_ref, gain_ref, row_ref, out_ref,
-    wbuf, wout, tok, qkv, outs, local, incoming, state_out, state_got, row, col, tail_out, tail_got,
+    n, nh, groups, tok_ref, w_ref, gain_ref, row_ref, out_ref, wbufs, wouts, tok, qkv, outs, local, incoming, state_out, state_got, row, col, tail_out, tail_got,
     x_send, x_recv, z_send, z_recv, y_send, y_recv,
     tok_send, tok_recv, tok_own, px_send, px_recv, ph_send, ph_recv,
     st_send, st_recv, tl_send, tl_recv, row_send, row_recv, out_send, out_recv, out_own,
@@ -33,11 +36,11 @@
     pairs = n // 2
     span = n // 8
     rows, width = tok_ref.shape[0], tok_ref.shape[1]
-    cols = wbuf.shape[-1]
-    depth = n * wbuf.shape[-2]
-    heads = cols // HEAD_DIM
+    depth = n * w_ref.shape[1]
+    all_heads = w_ref.shape[2] // 2 // HEAD_DIM
+    heads = groups[0][2]
+    halves = all_heads // heads
     chunks = rows // CHUNK
-    groups = groups_of(halves)
     last = len(groups) - 1
     ctx, head = lax.axis_index("ctx"), lax.axis_index("head")
     a, b, c = ctx // 4, (ctx // 2) % 2, ctx % 2
@@ -49,11 +52,12 @@
     def line_at(step):
         return lax.rem(a - step + lines, lines)
 
-    for g, (which, half) in enumerate(groups):
-        keep = pl.ds(pl.multiple_of((c * halves + half) * cols, 128), cols)
-        give = pl.ds(pl.multiple_of(((1 - c) * halves + half) * cols, 128), cols)
-        wbuf[g, a, b, c] = w_ref[which, :, keep]
-        wout[g] = w_ref[which, :, give]
+    for g, (which, first, count) in enumerate(groups):
+        span_of = count * HEAD_DIM
+        keep = pl.ds(pl.multiple_of((c * all_heads + first) * HEAD_DIM, 128), span_of)
+        give = pl.ds(pl.multiple_of(((1 - c) * all_heads + first) * HEAD_DIM, 128), span_of)
+        wbufs[g][a, b, c] = w_ref[which, :, keep]
+        wouts[g][...] = w_ref[which, :, give]
     row[c] = row_ref[...]
 
     barrier = pltpu.get_barrier_semaphore()
@@ -87,16 +91,16 @@
 
     def x_copy(g, c_):
         return remote(
-            wout.at[g], wbuf.at[g, a, b, c_], x_send.at[g], x_recv.at[g], place(a, b, 1 - c)
+            wouts[g], wbufs[g].at[a, b, c_], x_send.at[g], x_recv.at[g], place(a, b, 1 - c)
         )
 
     def z_copy(g, d, far, slot_line, to_line):
-        slot = wbuf.at[g, slot_line, b, 1 - c if far else c]
+        slot = wbufs[g].at[slot_line, b, 1 - c if far else c]
         at = d - 1 + (lines - 1 if far else 0)
         return remote(slot, slot, z_send.at[g, at], z_recv.at[g, at], place(to_line, b, c))
 
     def y_copy(g, k, far, b_):
-        slot = wbuf.at[g, line_at(k), b_, 1 - c if far else c]
+        slot = wbufs[g].at[line_at(k), b_, 1 - c if far else c]
         at = k + (lines if far else 0)
         return remote(slot, slot, y_send.at[g, at], y_recv.at[g, at], place(a, 1 - b, c))
 
@@ -139,19 +143,23 @@
     def row_copy(c_):
         return remote(row.at[c_], row.at[c_], row_send, row_recv, place(a, b, 1 - c))
 
-    def out_copy(half, i, of):
-        part = pl.ds(half * cols, cols)
-        there = pl.ds(pl.multiple_of((of * halves + half) * cols, 128), cols)
+    def lanes_of(g):
+        return pl.ds(groups[g][1] * HEAD_DIM, groups[g][2] * HEAD_DIM)
+
+    def out_lanes(g, of):
+        start = pl.multiple_of((of * all_heads + groups[g][1]) * HEAD_DIM, 128)
+        return pl.ds(start, groups[g][2] * HEAD_DIM)
+
+    def out_copy(g, i, of):
         at = pl.ds(pl.multiple_of(i * CHUNK, CHUNK), CHUNK)
         return remote(
-            outs.at[piece(1 - c, i), part], out_ref.at[at, there],
-            out_send.at[half, i], out_recv.at[half, i], place(a, b, 1 - c),
-        )
-
-    def out_keep(half):
-        there = pl.ds(pl.multiple_of((c * halves + half) * cols, 128), cols)
+            outs.at[piece(1 - c, i), lanes_of(g)], out_ref.at[at, out_lanes(g, of)],
+            out_send.at[g, i], out_recv.at[g, i], place(a, b, 1 - c),
+        )
+
+    def out_keep(g):
         return pltpu.make_async_copy(
-            outs.at[own_rows(c), pl.ds(half * cols, cols)], out_ref.at[:, there], out_own.at[half]
+            outs.at[own_rows(c), lanes_of(g)], out_ref.at[:, out_lanes(g, c)], out_own.at[g]
         )
 
     def next_head(d):
@@ -168,17 +176,22 @@
             z_copy(g, d, far, a, lax.rem(a + d, lines)).start()
 
     def begin(g):
-        x_copy(g, c).start()
-        spread(g, False)
+        if g <= last:
+            x_copy(g, c).start()
+
+    def own_part(g):
+        if g <= last:
+            spread(g, False)
 
     def pass_partner(g):
-        x_copy(g, 1 - c).wait_recv()
-        spread(g, True)
+        if g <= last:
+            x_copy(g, 1 - c).wait_recv()
+            spread(g, True)
 
     def pass_lines(g):
-        @pl.loop(1, lines)
-        def _(d):
-            for far in (False, True):
+        for far in (False, True):
+            @pl.loop(1, lines if g <= last else 1)
+            def _(d):
                 z_copy(g, d, far, line_at(d), a).wait_recv()
                 y_copy(g, d, far, b).start()
 
@@ -189,13 +202,13 @@
                 y_copy(g, d, far, 1 - b).wait_recv()
 
     def project(g, of, i, height):
-        which, half = groups[g]
+        which = groups[g][0]
         part = pl.ds(pl.multiple_of(of * rows + i * height, height), height)
-        got = dot(tok[part, :], wbuf[g].reshape(depth, cols)).astype(BF16)
+        got = dot(tok[part, :], wbufs[g][...].reshape(depth, groups[g][2] * HEAD_DIM)).astype(BF16)
         if which < 2:
             wide = got.astype(F32)
             got = jnp.where(wide > 0.0, wide + 1.0, jnp.exp(jnp.minimum(wide, 0.0))).astype(BF16)
-        qkv[which, part, half * cols:(half + 1) * cols] = got
+        qkv[which, part, lanes_of(g)] = got
 
     def project_own(g):
         @pl.loop(0, rows // 512)
@@ -234,26 +247,28 @@
         def _(j):
             state_copy(half, j).start()
 
-    def add_states():
+    def add_states(half):
         first = least(ids_of(0))
-        incoming[...] = jnp.zeros_like(incoming)
+        own = range(half * heads, (half + 1) * heads)
+        for at in own:
+            incoming[at] = jnp.zeros((HEAD_DIM, HEAD_DIM), F32)
 
         @pl.loop(0, span)
         def _(j):
-            tail_copy(j).wait_recv()
-            for half in range(halves):
-                state_copy(half, j).wait_recv()
+            if half == 0:
+                tail_copy(j).wait_recv()
+            state_copy(half, j).wait_recv()
             ids = tail_got[j][0:1, :] + jnp.where(pair > j, 0, -1000)
             linked = ids == first
-            for at in range(halves * heads):
+            for at in own:
                 incoming[at] += jnp.where(linked, state_got[j, at].astype(F32), 0.0)
 
         for i in range(2 * chunks):
             here = least(ids_of(i))
-            for at in range(halves * heads):
+            for at in own:
                 local[i, at] += jnp.where(here == first, incoming[at], 0.0)
 
-    def attend(half, of, i):
+    def attend(g, of, i):
         part = piece(of, i)
         ids_row = row[of, :, pl.ds(pl.multiple_of(i * CHUNK, CHUNK), CHUNK)]
         ids_col = col[part, 0:1]
@@ -261,8 +276,7 @@
         sooner = lax.broadcasted_iota(jnp.int32, (CHUNK, CHUNK), 1)
         visible = (sooner <= later) & (ids_row == ids_col)
         reached = ids_col == least(ids_row)
-        for h in range(heads):
-            at = half * heads + h
+        for at in range(groups[g][1], groups[g][1] + groups[g][2]):
             lanes = pl.ds(at * HEAD_DIM, HEAD_DIM)
             query = qkv[0, part, lanes]
             scores = dot(query, qkv[1, part, lanes], ((1,), (1,)))
@@ -271,23 +285,60 @@
             prefix = dot(query, local[of * chunks + i, at].astype(BF16))
             total = total + jnp.where(reached, prefix, 0.0)
             scale = lax.rsqrt(jnp.mean(total * total, axis=1, keepdims=True) + 1e-05)
-            gain = gain_ref[:, pl.ds(pl.multiple_of((c * halves * heads + at) * HEAD_DIM, 128), HEAD_DIM)]
+            gain = gain_ref[:, pl.ds(pl.multiple_of((c * all_heads + at) * HEAD_DIM, 128), HEAD_DIM)]
             outs[part, lanes] = (total * scale * gain).astype(BF16)
 
-    def attend_all(half):
-        @pl.loop(0, chunks)
+    def attend_partner(g, fresh):
+        @pl.loop(0, rows // 512)
         def _(i):
-            attend(half, 1 - c, i)
-            out_copy(half, i, c).start()
-
-        @pl.loop(0, chunks)
+            if fresh:
+                project(g, 1 - c, i, 512)
+            for part in range(512 // CHUNK):
+                attend(g, 1 - c, i * (512 // CHUNK) + part)
+            for part in range(512 // CHUNK):
+                out_copy(g, i * (512 // CHUNK) + part, c).start()
+
+    def attend_own(g, fresh):
+        @pl.loop(0, rows // 512)
         def _(i):
-            attend(half, c, i)
-
-        out_keep(half).start()
-
-    begin(0)
-    row_copy(c).start()
+            if fresh:
+                project(g, c, i, 512)
+            for part in range(512 // CHUNK):
+                attend(g, c, i * (512 // CHUNK) + part)
+
+        out_keep(g).start()
+
+    def pass_piece(i):
+        px_copy(i, 1 - c).wait_recv()
+
+        @pl.loop(1, nh)
+        def _(d):
+            ph_copy(i, d, head, next_head(d)).start()
+
+    def use_piece(i, of_groups):
+        @pl.loop(1, nh)
+        def _(d):
+            ph_copy(i, d, prior_head(d), head).wait_recv()
+
+        for g in of_groups:
+            project(g, 1 - c, i, CHUNK)
+
+    def project_pieces(g, count):
+        @pl.loop(0, count)
+        def _(i):
+            project(g, 1 - c, i, CHUNK)
+
+    def serve(g):
+        begin(g + 3)
+        if g + 1 < chunks:
+            px_copy(g + 1, c).start()
+        own_part(g + 2)
+        pass_partner(g + 2)
+        pass_lines(g + 1)
+
+    for g in range(3):
+        begin(g)
+    own_part(0)
 
     @pl.loop(1, nh)
     def _(d):
@@ -295,10 +346,11 @@
 
     own = pltpu.make_async_copy(tok_ref, tok.at[own_rows(c), features(head)], tok_own)
     own.start()
-    begin(1)
-    begin(2)
+    row_copy(c).start()
     px_copy(0, c).start()
     pass_partner(0)
+    own_part(1)
+    pass_lines(0)
     pass_partner(1)
     row_copy(1 - c).wait_recv()
     tail_out[...] = jnp.broadcast_to(most(row[1]), tail_out.shape)
@@ -309,58 +361,61 @@
 
     for i in range(2 * chunks):
         col[pl.ds(i * CHUNK, CHUNK), :] = jnp.broadcast_to(ids_of(i), (HEAD_DIM, CHUNK)).T
-    pass_lines(0)
-
-    for g in range(last + 1):
-        if g + 3 <= last:
-            begin(g + 3)
-        if g <= last - 2:
-            for i in range(g + 1, chunks if g == last - 2 else min(g + 2, chunks)):
+
+    serve(0)
+    own.wait()
+
+    @pl.loop(1, nh)
+    def _(d):
+        tok_copy(d, prior_head(d), head).wait_recv()
+
+    finish(0)
+    project_own(0)
+    serve(1)
+    if halves == 1:
+        for i in range(3, chunks):
+            px_copy(i, c).start()
+        finish(1)
+        project_own(1)
+        for i in range(chunks):
+            pass_piece(i)
+            use_piece(i, (0, 1))
+        own_states(0)
+        add_states(0)
+        queries = (2,)
+    else:
+        for g in range(1, 4):
+            if g > 1:
+                serve(g)
+            pass_piece(g - 1)
+            finish(g)
+            project_own(g)
+            if g > 1:
+                project_pieces(g, g - 1)
+            use_piece(g - 1, range(g + 1))
+        for i in range(3, chunks):
+            if i > 3:
                 px_copy(i, c).start()
-        if g + 2 <= last:
-            pass_partner(g + 2)
-        if g + 1 <= last:
-            pass_lines(g + 1)
-        if g == 0:
-            own.wait()
-
-            @pl.loop(1, nh)
-            def _(d):
-                tok_copy(d, prior_head(d), head).wait_recv()
-
-        if g == last:
-            ready, fresh = chunks, ()
-        else:
-            ready = min(max(g - 1, 0), chunks)
-            fresh = range(ready, chunks if g == last - 1 else min(g, chunks))
-        for i in fresh:
-            px_copy(i, 1 - c).wait_recv()
-
-            @pl.loop(1, nh)
-            def _(d):
-                ph_copy(i, d, head, next_head(d)).start()
-
+            pass_piece(i)
+        serve(4)
+        for i in range(3, chunks):
+            use_piece(i, range(4))
+        own_states(0)
+        add_states(0)
+        attend_partner(2, False)
+        serve(5)
+        attend_own(2, False)
+        finish(4)
+        project_own(4)
+        project_pieces(4, chunks)
+        own_states(1)
+        queries = (5, 6)
+    for g in queries:
         finish(g)
-        project_own(g)
-        if ready > 0:
-            @pl.loop(0, ready)
-            def _(i):
-                project(g, 1 - c, i, CHUNK)
-
-        for i in fresh:
-            @pl.loop(1, nh)
-            def _(d):
-                ph_copy(i, d, prior_head(d), head).wait_recv()
-
-            for earlier in range(g + 1):
-                project(earlier, 1 - c, i, CHUNK)
-        if g == last - 1:
-            for half in range(halves):
-                own_states(half)
-            add_states()
-            for half in range(halves - 1):
-                attend_all(half)
-    attend_all(halves - 1)
+        if g == 5:
+            add_states(1)
+        attend_partner(g, True)
+        attend_own(g, True)
 
     for g in range(last + 1):
         x_copy(g, c).wait_send()
@@ -394,38 +449,40 @@
         for half in range(halves):
             state_copy(half, j).wait_send()
 
-    for half in range(halves):
-        out_keep(half).wait()
-
-        @pl.loop(0, chunks)
-        def _(i):
-            out_copy(half, i, c).wait_send()
-            out_copy(half, i, 1 - c).wait_recv()
+    for g, (which, _, _) in enumerate(groups):
+        if which == 0:
+            out_keep(g).wait()
+
+            @pl.loop(0, chunks)
+            def _(i):
+                out_copy(g, i, c).wait_send()
+                out_copy(g, i, 1 - c).wait_recv()
 
 
 def per_device(n, nh, tokens, w_qkv, out_gain, seg_ids):
     rows, width = tokens.shape
     part_rows, own_cols = w_qkv.shape[1:]
-    halves = 2 if own_cols >= 4 * HEAD_DIM else 1
-    cols = own_cols // (2 * halves)
-    heads = own_cols // 2 // HEAD_DIM
+    cols = own_cols // 2
+    heads = cols // HEAD_DIM
+    plan = groups_of(heads)
+    halves = heads // plan[0][2]
     lines, span, chunks = n // 4, n // 8, rows // CHUNK
-    groups = 3 * halves
+    groups = len(plan)
     vmem = pl.BlockSpec(memory_space=pltpu.VMEM)
     hbm = pl.BlockSpec(memory_space=pl.ANY)
     dma = pltpu.SemaphoreType.DMA
     state = (heads, HEAD_DIM, HEAD_DIM)
     return pl.pallas_call(
-        functools.partial(kernel, n, nh, halves),
+        functools.partial(kernel, n, nh, plan),
         out_shape=jax.ShapeDtypeStruct((rows, own_cols), BF16),
         in_specs=[hbm, vmem, vmem, vmem],
         out_specs=hbm,
         scratch_shapes=[
-            pltpu.VMEM((groups, lines, 2, 2, part_rows, cols), BF16),
-            pltpu.VMEM((groups, part_rows, cols), BF16),
+            [pltpu.VMEM((lines, 2, 2, part_rows, count * HEAD_DIM), BF16) for _, _, count in plan],
+            [pltpu.VMEM((part_rows, count * HEAD_DIM), BF16) for _, _, count in plan],
             pltpu.VMEM((2 * rows, width * nh), BF16),
-            pltpu.VMEM((3, 2 * rows, halves * cols), BF16),
-            pltpu.VMEM((2 * rows, halves * cols), BF16),
+            pltpu.VMEM((3, 2 * rows, cols), BF16),
+            pltpu.VMEM((2 * rows, cols), BF16),
             pltpu.VMEM((2 * chunks,) + state, F32),
             pltpu.VMEM(state, F32),
             pltpu.VMEM(state, BF16),
@@ -443,7 +500,7 @@
             dma((halves, span)), dma((halves, span)),
             dma((span,)), dma((span,)),
             dma, dma,
-            dma((halves, chunks)), dma((halves, chunks)), dma((halves,)),
+            dma((groups, chunks)), dma((groups, chunks)), dma((groups,)),
         ],
         compiler_params=pltpu.CompilerParams(
             collective_id=0, has_side_effects=True, vmem_limit_bytes=56 * 1024 * 1024

time: 124 us -> 115 us (0.927)
  Pallas kernels: 121 us -> 112 us
    pallas_call x1, Pallas kernels: 121 us -> 112 us  [per_device(): pl.pallas_call(functools.partial(kernel, n, nh, plan), out_shape=jax.Shap...]
where the time goes in v3:
time: 115 us
  Pallas kernels  112 us (97%)
  local copies, waits for them, and re-layouts  3.08 us (3%)
    pallas_call x1, Pallas kernels, per_device(): pl.pallas_call(functools.partial(kernel, n, nh, plan), out_shape=jax.Shap...  112 us
    unnamed x1, local copies, waits for them, and re-layouts  3.08 us

profile of v3, /device:TPU:0, one launch (start us, length us, event | category | flops | bytes accessed | tf_op | source)
XLA Modules:
  0.0 115.2 jit_solution(17005365160961727845)
XLA Ops:
  0.0 112.1 %shard_map.46 = bf16[1024,1024]{1,0:T(8,128)(2,1)} custom-call(bf16[1024,1024]{1,0:T(8,128)(2,1)} %tok_ref.1, bf16[3,128,1024]{2,1,0:T(8,128)(2,1)} %w_ref.1, f32[1,1024]{1,0:T(1,128)} %bitcast.2, s32[1,1024]{1,0:T(1,128)} %bitcast.3), custom_call_target="tpu_custom_call" | custom-call | flops 12884901888 | bytes 4194304 | tf_op jit(solution)/shard_map/pallas_call | solution.py:475
  112.1 3.1 %copy.6 = bf16[1024,1024]{1,0:T(8,128)(2,1)} copy(bf16[1024,1024]{1,0:T(8,128)(2,1)} %shard_map.46) | data formatting | bytes 4194304

commit v4 on v3

--- a/solution.py
+++ b/solution.py
@@ -27,7 +27,7 @@
 
 
 def kernel(
-    n, nh, groups, tok_ref, w_ref, gain_ref, row_ref, out_ref, wbufs, wouts, tok, qkv, outs, local, incoming, state_out, state_got, row, col, tail_out, tail_got,
+    n, nh, groups, tok_ref, w_ref, gain_ref, row_ref, out_ref, wbufs, wouts, tok, qkv, outs, early, outers, local, incoming, state_out, state_got, row, col, tail_out, tail_got,
     x_send, x_recv, z_send, z_recv, y_send, y_recv,
     tok_send, tok_recv, tok_own, px_send, px_recv, ph_send, ph_recv,
     st_send, st_recv, tl_send, tl_recv, row_send, row_recv, out_send, out_recv, out_own,
@@ -52,6 +52,27 @@
     def line_at(step):
         return lax.rem(a - step + lines, lines)
 
+    barrier = pltpu.get_barrier_semaphore()
+
+    def greet(where):
+        pl.semaphore_signal(barrier, inc=1, device_id=where, device_id_type=MESH)
+
+    greet(place(a, b, 1 - c))
+    greet(place(a, 1 - b, c))
+
+    @pl.loop(1, lines)
+    def _(d):
+        greet(place(lax.rem(a + d, lines), b, c))
+
+    @pl.loop(1, span + 1)
+    def _(d):
+        greet((lax.rem(pair + d, pairs) * 2 + c, head))
+        greet((lax.rem(pair - d + pairs, pairs) * 2 + c, head))
+
+    @pl.loop(1, nh)
+    def _(d):
+        greet((ctx, lax.rem(head + d, nh)))
+
     for g, (which, first, count) in enumerate(groups):
         span_of = count * HEAD_DIM
         keep = pl.ds(pl.multiple_of((c * all_heads + first) * HEAD_DIM, 128), span_of)
@@ -59,27 +80,6 @@
         wbufs[g][a, b, c] = w_ref[which, :, keep]
         wouts[g][...] = w_ref[which, :, give]
     row[c] = row_ref[...]
-
-    barrier = pltpu.get_barrier_semaphore()
-
-    def greet(where):
-        pl.semaphore_signal(barrier, inc=1, device_id=where, device_id_type=MESH)
-
-    greet(place(a, b, 1 - c))
-    greet(place(a, 1 - b, c))
-
-    @pl.loop(1, lines)
-    def _(d):
-        greet(place(lax.rem(a + d, lines), b, c))
-
-    @pl.loop(1, span + 1)
-    def _(d):
-        greet((lax.rem(pair + d, pairs) * 2 + c, head))
-        greet((lax.rem(pair - d + pairs, pairs) * 2 + c, head))
-
-    @pl.loop(1, nh)
-    def _(d):
-        greet((ctx, lax.rem(head + d, nh)))
 
     pl.semaphore_wait(barrier, 2 + (lines - 1) + 2 * span + (nh - 1))
 
@@ -224,22 +224,32 @@
     def most(ids):
         return jnp.max(ids, axis=1, keepdims=True)
 
+    def outer(half, of, i):
+        part = piece(of, i)
+        tail = most(row[of, :, pl.ds(pl.multiple_of(i * CHUNK, CHUNK), CHUNK)])
+        in_tail = col[part, 0:1] == tail
+        for at in range(half * heads, (half + 1) * heads):
+            lanes = pl.ds(at * HEAD_DIM, HEAD_DIM)
+            keys = qkv[1, part, lanes]
+            keys = jnp.where(in_tail, keys, jnp.zeros_like(keys))
+            outers[of * chunks + i, at] = dot(keys, qkv[2, part, lanes], ((0,), (0,)))
+
+    def outer_all(half, of):
+        @pl.loop(0, chunks)
+        def _(i):
+            outer(half, of, i)
+
     def own_states(half):
         for h in range(heads):
             at = half * heads + h
-            lanes = pl.ds(at * HEAD_DIM, HEAD_DIM)
             state = jnp.zeros((HEAD_DIM, HEAD_DIM), F32)
             before = None
             for i in range(2 * chunks):
-                part = pl.ds(i * CHUNK, CHUNK)
                 first, tail = least(ids_of(i)), most(ids_of(i))
                 if i > 0:
                     state = jnp.where(before == first, state, 0.0)
                 local[i, at] = state
-                keys = qkv[1, part, lanes]
-                keys = jnp.where(col[part, 0:1] == tail, keys, jnp.zeros_like(keys))
-                fresh = dot(keys, qkv[2, part, lanes], ((0,), (0,)))
-                state = jnp.where(first == tail, state, 0.0) + fresh
+                state = jnp.where(first == tail, state, 0.0) + outers[i, at]
                 before = tail
             state_out[at] = state.astype(BF16)
 
@@ -268,21 +278,38 @@
             for at in own:
                 local[i, at] += jnp.where(here == first, incoming[at], 0.0)
 
-    def attend(g, of, i):
+    def heads_of(g):
+        return range(groups[g][1], groups[g][1] + groups[g][2])
+
+    def local_parts(g, of, i):
         part = piece(of, i)
         ids_row = row[of, :, pl.ds(pl.multiple_of(i * CHUNK, CHUNK), CHUNK)]
-        ids_col = col[part, 0:1]
         later = lax.broadcasted_iota(jnp.int32, (CHUNK, CHUNK), 0)
         sooner = lax.broadcasted_iota(jnp.int32, (CHUNK, CHUNK), 1)
-        visible = (sooner <= later) & (ids_row == ids_col)
-        reached = ids_col == least(ids_row)
-        for at in range(groups[g][1], groups[g][1] + groups[g][2]):
+        visible = (sooner <= later) & (ids_row == col[part, 0:1])
+        totals = []
+        for at in heads_of(g):
             lanes = pl.ds(at * HEAD_DIM, HEAD_DIM)
-            query = qkv[0, part, lanes]
-            scores = dot(query, qkv[1, part, lanes], ((1,), (1,)))
+            scores = dot(qkv[0, part, lanes], qkv[1, part, lanes], ((1,), (1,)))
             scores = jnp.where(visible, scores, 0.0).astype(BF16)
-            total = dot(scores, qkv[2, part, lanes])
-            prefix = dot(query, local[of * chunks + i, at].astype(BF16))
+            totals.append(dot(scores, qkv[2, part, lanes]))
+        return totals
+
+    def keep_local(g, of, i):
+        for at, total in zip(heads_of(g), local_parts(g, of, i)):
+            early[piece(of, i), pl.ds(at * HEAD_DIM, HEAD_DIM)] = total
+
+    def attend(g, of, i, fresh):
+        part = piece(of, i)
+        ids_row = row[of, :, pl.ds(pl.multiple_of(i * CHUNK, CHUNK), CHUNK)]
+        reached = col[part, 0:1] == least(ids_row)
+        if fresh:
+            totals = local_parts(g, of, i)
+        else:
+            totals = [early[part, pl.ds(at * HEAD_DIM, HEAD_DIM)] for at in heads_of(g)]
+        for at, total in zip(heads_of(g), totals):
+            lanes = pl.ds(at * HEAD_DIM, HEAD_DIM)
+            prefix = dot(qkv[0, part, lanes], local[of * chunks + i, at].astype(BF16))
             total = total + jnp.where(reached, prefix, 0.0)
             scale = lax.rsqrt(jnp.mean(total * total, axis=1, keepdims=True) + 1e-05)
             gain = gain_ref[:, pl.ds(pl.multiple_of((c * all_heads + at) * HEAD_DIM, 128), HEAD_DIM)]
@@ -294,7 +321,7 @@
             if fresh:
                 project(g, 1 - c, i, 512)
             for part in range(512 // CHUNK):
-                attend(g, 1 - c, i * (512 // CHUNK) + part)
+                attend(g, 1 - c, i * (512 // CHUNK) + part, fresh)
             for part in range(512 // CHUNK):
                 out_copy(g, i * (512 // CHUNK) + part, c).start()
 
@@ -304,7 +331,7 @@
             if fresh:
                 project(g, c, i, 512)
             for part in range(512 // CHUNK):
-                attend(g, c, i * (512 // CHUNK) + part)
+                attend(g, c, i * (512 // CHUNK) + part, fresh)
 
         out_keep(g).start()
 
@@ -380,6 +407,8 @@
         for i in range(chunks):
             pass_piece(i)
             use_piece(i, (0, 1))
+        outer_all(0, c)
+        outer_all(0, 1 - c)
         own_states(0)
         add_states(0)
         queries = (2,)
@@ -392,7 +421,18 @@
             project_own(g)
             if g > 1:
                 project_pieces(g, g - 1)
+            if g == 1:
+                outer_all(0, c)
+            elif g == 2:
+                @pl.loop(0, chunks)
+                def _(i):
+                    keep_local(2, c, i)
+
+                keep_local(2, 1 - c, 0)
             use_piece(g - 1, range(g + 1))
+            outer(0, 1 - c, g - 1)
+            if g > 1:
+                keep_local(2, 1 - c, g - 1)
         for i in range(3, chunks):
             if i > 3:
                 px_copy(i, c).start()
@@ -400,6 +440,8 @@
         serve(4)
         for i in range(3, chunks):
             use_piece(i, range(4))
+            outer(0, 1 - c, i)
+            keep_local(2, 1 - c, i)
         own_states(0)
         add_states(0)
         attend_partner(2, False)
@@ -408,6 +450,8 @@
         finish(4)
         project_own(4)
         project_pieces(4, chunks)
+        outer_all(1, c)
+        outer_all(1, 1 - c)
         own_states(1)
         queries = (5, 6)
     for g in queries:
@@ -483,6 +527,8 @@
             pltpu.VMEM((2 * rows, width * nh), BF16),
             pltpu.VMEM((3, 2 * rows, cols), BF16),
             pltpu.VMEM((2 * rows, cols), BF16),
+            pltpu.VMEM((2 * rows, plan[0][2] * HEAD_DIM), F32),
+            pltpu.VMEM((2 * chunks,) + state, F32),
             pltpu.VMEM((2 * chunks,) + state, F32),
             pltpu.VMEM(state, F32),
             pltpu.VMEM(state, BF16),
@@ -503,7 +549,7 @@
             dma((groups, chunks)), dma((groups, chunks)), dma((groups,)),
         ],
         compiler_params=pltpu.CompilerParams(
-            collective_id=0, has_side_effects=True, vmem_limit_bytes=56 * 1024 * 1024
+            collective_id=0, has_side_effects=True, vmem_limit_bytes=44 * 1024 * 1024
         ),
         cost_estimate=pl.CostEstimate(
             flops=2 * rows * width * nh * own_cols * 3,

time: 115 us -> 117 us (1.017)
  local copies, waits for them, and re-layouts: 3.08 us -> 5.42 us
    unnamed x1 -> x9, local copies, waits for them, and re-layouts: 3.08 us -> 5.42 us
where the time goes in v4:
time: 117 us
  Pallas kernels  111 us (95%)
  local copies, waits for them, and re-layouts  5.42 us (5%)
    pallas_call x1, Pallas kernels, per_device(): pl.pallas_call(functools.partial(kernel, n, nh, plan), out_shape=jax.Shap...  111 us
    unnamed x9, local copies, waits for them, and re-layouts  5.42 us

profile of v4, /device:TPU:0, one launch (start us, length us, event | category | flops | bytes accessed | tf_op | source)
XLA Modules:
  0.0 116.5 jit_solution(1076654924023686377)
XLA Ops:
  0.0 0.0 copy-start
  0.0 1.6 %copy-done = bf16[1024,1024]{1,0:T(8,128)(2,1)S(1)} copy-done((bf16[1024,1024]{1,0:T(8,128)(2,1)S(1)}, bf16[1024,1024]{1,0:T(8,128)(2,1)}, u32[]{:S(2)}) %copy-start) | copy-done | bytes 2097176
  1.6 0.0 copy-start.1
  1.6 1.1 copy-done.1
  2.7 0.0 copy-start.2
  2.7 0.7 copy-done.2
  3.4 0.0 copy-start.3
  3.4 0.7 copy-done.3
  4.1 111.1 %shard_map.46 = bf16[1024,1024]{1,0:T(8,128)(2,1)S(1)} custom-call(bf16[1024,1024]{1,0:T(8,128)(2,1)S(1)} %copy-done, bf16[3,128,1024]{2,1,0:T(8,128)(2,1)S(1)} %copy-done.1, f32[1,1024]{1,0:T(1,128)S(1)} %bitcast.2, s32[1,1024]{1,0:T(1,128)S(1)} %bitcast.3), custom_call_target="tpu_custom_call" | custom-call | flops 12884901888 | bytes 4194304 | tf_op jit(solution)/shard_map/pallas_call | solution.py:519
  115.2 1.3 %copy.6 = bf16[1024,1024]{1,0:T(8,128)(2,1)} copy(bf16[1024,1024]{1,0:T(8,128)(2,1)S(1)} %shard_map.46) | data formatting | bytes 4194304
Async XLA Ops:
  0.0 1.6 %copy-start = (bf16[1024,1024]{1,0:T(8,128)(2,1)S(1)}, bf16[1024,1024]{1,0:T(8,128)(2,1)}, u32[]{:S(2)}) copy-start(bf16[1024,1024]{1,0:T(8,128)(2,1)} %tok_ref.1) | copy-start | bytes 6291460
  1.6 1.1 copy-start.1
  2.7 0.7 copy-start.2
  3.4 0.7 copy-start.3

commit v5 on v4

--- a/solution.py
+++ b/solution.py
@@ -188,12 +188,23 @@
             x_copy(g, 1 - c).wait_recv()
             spread(g, True)
 
-    def pass_lines(g):
-        for far in (False, True):
-            @pl.loop(1, lines if g <= last else 1)
-            def _(d):
-                z_copy(g, d, far, line_at(d), a).wait_recv()
-                y_copy(g, d, far, b).start()
+    def line_steps(g):
+        def step(far, d):
+            z_copy(g, d, far, line_at(d), a).wait_recv()
+            y_copy(g, d, far, b).start()
+
+        return [
+            functools.partial(step, far, d) for far in (False, True) for d in range(1, lines)
+        ]
+
+    def weave(steps, tasks, at_once=1):
+        steps, tasks = list(steps), list(tasks)
+        while steps or tasks:
+            for step in steps[:at_once]:
+                step()
+            steps = steps[at_once:]
+            if tasks:
+                tasks.pop(0)()
 
     def finish(g):
         @pl.loop(0, lines)
@@ -361,7 +372,6 @@
             px_copy(g + 1, c).start()
         own_part(g + 2)
         pass_partner(g + 2)
-        pass_lines(g + 1)
 
     for g in range(3):
         begin(g)
@@ -377,7 +387,7 @@
     px_copy(0, c).start()
     pass_partner(0)
     own_part(1)
-    pass_lines(0)
+    weave(line_steps(0), ())
     pass_partner(1)
     row_copy(1 - c).wait_recv()
     tail_out[...] = jnp.broadcast_to(most(row[1]), tail_out.shape)
@@ -389,6 +399,9 @@
     for i in range(2 * chunks):
         col[pl.ds(i * CHUNK, CHUNK), :] = jnp.broadcast_to(ids_of(i), (HEAD_DIM, CHUNK)).T
 
+    def do(function, *args):
+        return functools.partial(function, *args)
+
     serve(0)
     own.wait()
 
@@ -396,14 +409,12 @@
     def _(d):
         tok_copy(d, prior_head(d), head).wait_recv()
 
-    finish(0)
-    project_own(0)
+    weave(line_steps(1), [do(finish, 0), do(project_own, 0)])
     serve(1)
     if halves == 1:
         for i in range(3, chunks):
             px_copy(i, c).start()
-        finish(1)
-        project_own(1)
+        weave(line_steps(2), [do(finish, 1), do(project_own, 1)])
         for i in range(chunks):
             pass_piece(i)
             use_piece(i, (0, 1))
@@ -413,46 +424,43 @@
         add_states(0)
         queries = (2,)
     else:
+        def keep_own(g):
+            @pl.loop(0, chunks)
+            def _(i):
+                keep_local(g, c, i)
+
         for g in range(1, 4):
             if g > 1:
                 serve(g)
             pass_piece(g - 1)
-            finish(g)
-            project_own(g)
+            tasks = [do(finish, g), do(project_own, g)]
             if g > 1:
-                project_pieces(g, g - 1)
+                tasks.append(do(project_pieces, g, g - 1))
             if g == 1:
-                outer_all(0, c)
+                tasks.append(do(outer_all, 0, c))
             elif g == 2:
-                @pl.loop(0, chunks)
-                def _(i):
-                    keep_local(2, c, i)
-
-                keep_local(2, 1 - c, 0)
-            use_piece(g - 1, range(g + 1))
-            outer(0, 1 - c, g - 1)
+                tasks += [do(keep_own, 2), do(keep_local, 2, 1 - c, 0)]
+            tasks += [do(use_piece, g - 1, range(g + 1)), do(outer, 0, 1 - c, g - 1)]
             if g > 1:
-                keep_local(2, 1 - c, g - 1)
+                tasks.append(do(keep_local, 2, 1 - c, g - 1))
+            weave(line_steps(g + 1), tasks)
         for i in range(3, chunks):
             if i > 3:
                 px_copy(i, c).start()
             pass_piece(i)
         serve(4)
+        tasks = []
         for i in range(3, chunks):
-            use_piece(i, range(4))
-            outer(0, 1 - c, i)
-            keep_local(2, 1 - c, i)
-        own_states(0)
-        add_states(0)
-        attend_partner(2, False)
-        serve(5)
-        attend_own(2, False)
-        finish(4)
-        project_own(4)
-        project_pieces(4, chunks)
-        outer_all(1, c)
-        outer_all(1, 1 - c)
-        own_states(1)
+            tasks += [
+                do(use_piece, i, range(4)), do(outer, 0, 1 - c, i), do(keep_local, 2, 1 - c, i)
+            ]
+        tasks += [
+            do(own_states, 0), do(finish, 4), do(project_own, 4), do(add_states, 0),
+            do(attend_partner, 2, False), do(project_pieces, 4, chunks),
+            do(outer_all, 1, c), do(outer_all, 1, 1 - c), do(own_states, 1),
+            do(attend_own, 2, False),
+        ]
+        weave(line_steps(5) + line_steps(6), tasks, 2)
         queries = (5, 6)
     for g in queries:
         finish(g)
@@ -549,7 +557,7 @@
             dma((groups, chunks)), dma((groups, chunks)), dma((groups,)),
         ],
         compiler_params=pltpu.CompilerParams(
-            collective_id=0, has_side_effects=True, vmem_limit_bytes=44 * 1024 * 1024
+            collective_id=0, has_side_effects=True, vmem_limit_bytes=56 * 1024 * 1024
         ),
         cost_estimate=pl.CostEstimate(
             flops=2 * rows * width * nh * own_cols * 3,

time: 117 us -> 117 us (level)
  local copies, waits for them, and re-layouts: 5.42 us -> 3.08 us
  Pallas kernels: 111 us -> 113 us
    unnamed x9 -> x1, local copies, waits for them, and re-layouts: 5.42 us -> 3.08 us
    pallas_call x1, Pallas kernels: 111 us -> 113 us  [per_device(): pl.pallas_call(functools.partial(kernel, n, nh, plan), out_shape=jax.Shap...]
where the time goes in v5:
time: 117 us; the launch traced here: 116 us
  Pallas kernels  113 us (97%)
  local copies, waits for them, and re-layouts  3.08 us (3%)
    pallas_call x1, Pallas kernels, per_device(): pl.pallas_call(functools.partial(kernel, n, nh, plan), out_shape=jax.Shap...  113 us
    unnamed x1, local copies, waits for them, and re-layouts  3.08 us

profile of v5, /device:TPU:0, one launch (start us, length us, event | category | flops | bytes accessed | tf_op | source)
XLA Modules:
  0.0 116.1 jit_solution(13811562625866988359)
XLA Ops:
  0.0 113.0 %shard_map.46 = bf16[1024,1024]{1,0:T(8,128)(2,1)} custom-call(bf16[1024,1024]{1,0:T(8,128)(2,1)} %tok_ref.1, bf16[3,128,1024]{2,1,0:T(8,128)(2,1)} %w_ref.1, f32[1,1024]{1,0:T(1,128)} %bitcast.2, s32[1,1024]{1,0:T(1,128)} %bitcast.3), custom_call_target="tpu_custom_call" | custom-call | flops 12884901888 | bytes 4194304 | tf_op jit(solution)/shard_map/pallas_call | solution.py:527
  113.0 3.1 %copy.6 = bf16[1024,1024]{1,0:T(8,128)(2,1)} copy(bf16[1024,1024]{1,0:T(8,128)(2,1)} %shard_map.46) | data formatting | bytes 4194304

commit v6 on v3

--- a/solution.py
+++ b/solution.py
@@ -94,10 +94,20 @@
             wouts[g], wbufs[g].at[a, b, c_], x_send.at[g], x_recv.at[g], place(a, b, 1 - c)
         )
 
-    def z_copy(g, d, far, slot_line, to_line):
-        slot = wbufs[g].at[slot_line, b, 1 - c if far else c]
-        at = d - 1 + (lines - 1 if far else 0)
-        return remote(slot, slot, z_send.at[g, at], z_recv.at[g, at], place(to_line, b, c))
+    def z_copy(g, origin, far, way):
+        slot = wbufs[g].at[origin, b, 1 - c if far else c]
+        at = origin + (lines if far else 0)
+        sent = at + (2 * lines if way > 0 else 0)
+        to_line = lax.rem(a + way + lines, lines)
+        return remote(slot, slot, z_send.at[g, sent], z_recv.at[g, at], place(to_line, b, c))
+
+    def z_both(g, origin_of, far, act):
+        for way in (1, -1):
+            origin = origin_of(-way)
+
+            @pl.when((origin >= 0) & (origin < lines) & (a + way >= 0) & (a + way < lines))
+            def _():
+                act(z_copy(g, lax.rem(origin + lines, lines), far, way))
 
     def y_copy(g, k, far, b_):
         slot = wbufs[g].at[line_at(k), b_, 1 - c if far else c]
@@ -171,9 +181,7 @@
     def spread(g, far):
         y_copy(g, 0, far, b).start()
 
-        @pl.loop(1, lines)
-        def _(d):
-            z_copy(g, d, far, a, lax.rem(a + d, lines)).start()
+        z_both(g, lambda side: a, far, lambda copy: copy.start())
 
     def begin(g):
         if g <= last:
@@ -192,8 +200,19 @@
         for far in (False, True):
             @pl.loop(1, lines if g <= last else 1)
             def _(d):
-                z_copy(g, d, far, line_at(d), a).wait_recv()
-                y_copy(g, d, far, b).start()
+                for way in (1, -1):
+                    origin = a - way * d
+
+                    @pl.when((origin >= 0) & (origin < lines))
+                    def _():
+                        at = lax.rem(origin + lines, lines)
+                        z_copy(g, at, far, way).wait_recv()
+
+                        @pl.when((a + way >= 0) & (a + way < lines))
+                        def _():
+                            z_copy(g, at, far, way).start()
+
+                        y_copy(g, lax.rem(a - origin + lines, lines), far, b).start()
 
     def finish(g):
         @pl.loop(0, lines)
@@ -420,10 +439,10 @@
     for g in range(last + 1):
         x_copy(g, c).wait_send()
 
-        @pl.loop(1, lines)
+        @pl.loop(0, lines)
         def _(d):
             for far in (False, True):
-                z_copy(g, d, far, a, lax.rem(a + d, lines)).wait_send()
+                z_both(g, lambda side: a + side * d, far, lambda copy: copy.wait_send())
 
         @pl.loop(0, lines)
         def _(d):
@@ -492,7 +511,7 @@
             pltpu.VMEM((8, HEAD_DIM), jnp.int32),
             pltpu.VMEM((span, 8, HEAD_DIM), jnp.int32),
             dma((groups,)), dma((groups,)),
-            dma((groups, 2 * lines - 2)), dma((groups, 2 * lines - 2)),
+            dma((groups, 4 * lines)), dma((groups, 2 * lines)),
             dma((groups, 2 * lines)), dma((groups, 2 * lines)),
             dma((nh - 1,)), dma((nh - 1,)), dma,
             dma((chunks,)), dma((chunks,)),

time: 115 us -> 122 us (1.061)
  Pallas kernels: 112 us -> 119 us
    pallas_call x1, Pallas kernels: 112 us -> 119 us  [per_device(): pl.pallas_call(functools.partial(kernel, n, nh, plan), out_shape=jax.Shap...]
where the time goes in v6:
time: 122 us
  Pallas kernels  119 us (98%)
  local copies, waits for them, and re-layouts  3.08 us (3%)
    pallas_call x1, Pallas kernels, per_device(): pl.pallas_call(functools.partial(kernel, n, nh, plan), out_shape=jax.Shap...  119 us
    unnamed x1, local copies, waits for them, and re-layouts  3.08 us

profile of v6, /device:TPU:0, one launch (start us, length us, event | category | flops | bytes accessed | tf_op | source)
XLA Modules:
  0.0 121.8 jit_solution(7833525232049564046)
XLA Ops:
  0.0 118.7 %shard_map.46 = bf16[1024,1024]{1,0:T(8,128)(2,1)} custom-call(bf16[1024,1024]{1,0:T(8,128)(2,1)} %tok_ref.1, bf16[3,128,1024]{2,1,0:T(8,128)(2,1)} %w_ref.1, f32[1,1024]{1,0:T(1,128)} %bitcast.2, s32[1,1024]{1,0:T(1,128)} %bitcast.3), custom_call_target="tpu_custom_call" | custom-call | flops 12884901888 | bytes 4194304 | tf_op jit(solution)/shard_map/pallas_call | solution.py:494
  118.8 3.1 %copy.6 = bf16[1024,1024]{1,0:T(8,128)(2,1)} copy(bf16[1024,1024]{1,0:T(8,128)(2,1)} %shard_map.46) | data formatting | bytes 4194304
